TPU v7x, 512 devices: a whole 4x4x16 slice. The times are simulated.
512 devices in a mesh: bx: 16 (over z_hi, y), by: 32 (over z_lo, x, core).
Axes of the slice: x: 4, y: 4, z: 16 (z_hi: 4, z_lo: 4; z = z_hi * 4 + z_lo), core: 2. Of those that a mesh axis runs over, the one named last changes fastest.
Arguments:
- density: float32 [512, 1024, 128], P('bx', 'by'), may hold values from 0 to 6
- band_feat: bfloat16 [16, 32, 4, 2048, 64], P('bx', 'by'), may hold values from -6 to 6
- band_cell: int32 [16, 32, 4, 2048], P('bx', 'by'), may hold values from 0 to 131071, as said below
- band_count: int32 [16, 32, 4], P('bx', 'by'), may hold values from 1024 to 2048, as said below
- w_in: bfloat16 [16, 32, 64, 256], P('bx', 'by'), may hold values from -0.75 to 0.75
- w_hid: bfloat16 [16, 32, 4, 256, 256], P('bx', 'by'), may hold values from -0.5 to 0.5
- w_out: bfloat16 [16, 32, 256], P('bx', 'by'), may hold values from -0.5 to 0.5
- biases: float32 [16, 32, 5, 256], P('bx', 'by'), may hold values from -2 to 2
Outputs:
- smoothed: float32 [512, 1024, 128], P('bx', 'by')
- normals: float32 [3, 512, 1024, 128], P(None, 'bx', 'by')
Inputs may be any that keep to these rules, and one draw needn't show every extreme that they name: `band_count`: every count is 1024 or more, and some side of some block reaches 2048. `band_cell`: the entries of one side of one block are voxels of that side's band, the 16 voxels next to the block's face: side 0 at the low end of the first dimension, 1 at its high end, 2 and 3 likewise along the second. Taking the band's voxels in row-major order of the band itself (first dimension, second, height) and cutting that order into 2048 equal consecutive runs, entry r lies in run r.
All inputs are finite; a program needn't handle non-finite values.
Results may differ from a plain program's by a relative error of at most 0.0008.
Values may be sent and summed in bfloat16 or wider, within the bound.
A program may use at most 64 MiB of HBM per device.

v0:
```python
import jax
import jax.numpy as jnp
from jax import lax
from jax.sharding import PartitionSpec as P

W = 16


OFFSETS = ((-1, 0), (1, 0), (0, -1), (0, 1))


def shifted(shard, axis, by):
    peers = lax.axis_size(axis)
    pairs = [(i, i + by) for i in range(peers) if 0 <= i + by < peers]
    return lax.ppermute(shard, axis, pairs)


def extended(shard, sides, width):
    for axis, dim in sides:
        peers, length = (lax.axis_size(axis), shard.shape[dim])
        up = [(i, (i + 1) % peers) for i in range(peers - 1)]
        down = [(j, i) for i, j in up]
        last = lax.slice_in_dim(shard, length - width, length, axis=dim)
        leading = lax.slice_in_dim(shard, 0, width, axis=dim)
        before = lax.ppermute(last, axis, up)
        after = lax.ppermute(leading, axis, down)
        shard = jnp.concatenate([before, shard, after], axis=dim)
    return shard


def network(features, w_in, w_hid, w_out, biases):
    hidden = jnp.maximum(
        jnp.dot(features, w_in, preferred_element_type=jnp.float32) + biases[0], 0.0
    ).astype(jnp.bfloat16)
    for levels in range(w_hid.shape[0]):
        hidden = jnp.maximum(
            jnp.dot(hidden, w_hid[levels], preferred_element_type=jnp.float32) + biases[levels + 1],
            0.0,
        ).astype(jnp.bfloat16)
    return jax.nn.softplus(jnp.dot(hidden, w_out, preferred_element_type=jnp.float32))


def weight_at(cell_index, tile_x, tile_y, tile_z, off_x, off_y):
    pos_x = (cell_index // (tile_y * tile_z)).astype(jnp.float32)
    pos_y = (cell_index // tile_z % tile_y).astype(jnp.float32)
    delta_x = (pos_x + 0.5) / tile_x - 0.5 - off_x
    delta_y = (pos_y + 0.5) / tile_y - 0.5 - off_y
    return 1.0 / (delta_x * delta_x + delta_y * delta_y + 0.25)


def smooth_once(padded):
    return (
        padded[1:-1, 1:-1]
        + padded[2:, 1:-1]
        + padded[:-2, 1:-1]
        + padded[1:-1, 2:]
        + padded[1:-1, :-2]
    ) / 5.0


def send_rows_x(features, offset):
    return shifted(features, "bx", offset)


def send_rows_y(features, offset):
    return shifted(features, "by", offset)


def back_dens_x(values, offset):
    return shifted(values, "bx", offset)


def back_dens_y(values, offset):
    return shifted(values, "by", offset)


def thin_rim(field_now):
    return extended(field_now, (("bx", 0), ("by", 1)), 1)


def band_spread(facing, cell_index, values_pair, tile_x, tile_y, tile_z):
    listed = cell_index.shape[0]
    if facing < 2:
        lift = 0 if facing == 0 else tile_x - W
        band_shape = (W, tile_y, tile_z)
        position = cell_index - lift * tile_y * tile_z
        widths = (
            ((0, tile_x - W), (0, 0), (0, 0)) if facing == 0 else ((tile_x - W, 0), (0, 0), (0, 0))
        )
    else:
        lift = 0 if facing == 2 else tile_y - W
        band_shape = (tile_x, W, tile_z)
        row_pos = cell_index // (tile_y * tile_z)
        col_pos = cell_index // tile_z % tile_y - lift
        height = cell_index % tile_z
        position = (row_pos * W + col_pos) * tile_z + height
        widths = (
            ((0, 0), (0, tile_y - W), (0, 0)) if facing == 2 else ((0, 0), (tile_y - W, 0), (0, 0))
        )
    slot = band_shape[0] * band_shape[1] * band_shape[2] // listed
    within = position - jnp.arange(listed, dtype=jnp.int32) * slot
    hits = within[:, None] == jnp.arange(slot, dtype=jnp.int32)[None, :]
    outputs = []
    for values in values_pair:
        band = jnp.where(hits, values[:, None], 0.0).reshape(band_shape)
        outputs.append(jnp.pad(band, widths))
    return outputs


def shards(density, band_feat, band_cell, band_count, w_in, w_hid, w_out, biases):
    tile_x, tile_y, tile_z = density.shape
    cells = tile_x * tile_y * tile_z
    features = band_feat[0, 0]
    cell_lists = band_cell[0, 0]
    counts = band_count[0, 0]
    own_net = (w_in[0, 0], w_hid[0, 0], w_out[0, 0], biases[0, 0])
    row_block = lax.axis_index("bx")
    col_block = lax.axis_index("by")
    rows_total = lax.axis_size("bx")
    cols_total = lax.axis_size("by")
    exists = [row_block > 0, row_block < rows_total - 1, col_block > 0, col_block < cols_total - 1]
    arrived = [
        send_rows_x(features[0], -1),
        send_rows_x(features[1], 1),
        send_rows_y(features[2], -1),
        send_rows_y(features[3], 1),
    ]
    evaluated = [network(rows_in, *own_net) for rows_in in arrived]
    remote = [
        back_dens_x(evaluated[0], 1),
        back_dens_x(evaluated[1], -1),
        back_dens_y(evaluated[2], 1),
        back_dens_y(evaluated[3], -1),
    ]
    every_cell = jnp.arange(cells, dtype=jnp.int32)
    own_weight = weight_at(every_cell, tile_x, tile_y, tile_z, 0.0, 0.0).reshape(
        tile_x, tile_y, tile_z
    )
    numerator = jnp.zeros((tile_x, tile_y, tile_z), jnp.float32)
    denominator = jnp.zeros((tile_x, tile_y, tile_z), jnp.float32)
    ranks = jnp.arange(cell_lists.shape[1], dtype=jnp.int32)
    for facing in range(4):
        off_x, off_y = OFFSETS[facing]
        cell_index = cell_lists[facing]
        usable = (ranks < counts[facing]) & exists[facing]
        weight = jnp.where(
            usable, weight_at(cell_index, tile_x, tile_y, tile_z, float(off_x), float(off_y)), 0.0
        )
        num_band, den_band = band_spread(
            facing, cell_index, (weight * remote[facing], weight), tile_x, tile_y, tile_z
        )
        numerator = numerator + num_band
        denominator = denominator + den_band
    blended = (own_weight * density + numerator) / (own_weight + denominator)
    smoothed = blended
    for passes in range(3):
        smoothed = smooth_once(thin_rim(smoothed))
    padded = thin_rim(smoothed)
    grad_x = padded[2:, 1:-1] - padded[:-2, 1:-1]
    grad_y = padded[1:-1, 2:] - padded[1:-1, :-2]
    padded_z = jnp.pad(smoothed, ((0, 0), (0, 0), (1, 1)))
    grad_z = padded_z[:, :, 2:] - padded_z[:, :, :-2]
    factor = 1.0 / jnp.sqrt(1.0 + grad_x * grad_x + grad_y * grad_y + grad_z * grad_z)
    normals = jnp.stack([grad_x * factor, grad_y * factor, grad_z * factor])
    return (smoothed, normals)


def solution(mesh):
    placed = (
        P("bx", "by", None),
        P("bx", "by", None, None, None),
        P("bx", "by", None, None),
        P("bx", "by", None),
        P("bx", "by", None, None),
        P("bx", "by", None, None, None),
        P("bx", "by", None),
        P("bx", "by", None, None),
    )
    return jax.shard_map(
        shards,
        mesh=mesh,
        in_specs=placed,
        out_specs=(P("bx", "by", None), P(None, "bx", "by", None)),
        check_vma=False,
    )
```

profile of v0, /device:TPU:416, one launch (start us, length us, event | category | flops | bytes accessed | tf_op | source)
XLA Modules:
  0.0 193.8 jit_solution(15182307272058674744)
XLA Ops:
  2.7 7.9 %collective-permute-start = (bf16[2048,64]{0,1:T(8,128)(2,1)}, bf16[2048,64]{0,1:T(8,128)(2,1)}, u32[]{:S(2)}, u32[]{:S(2)}) collective-permute-start(bf16[2048,64]{0,1:T(8,128)(2,1)} %get-tuple-element.18), channel_id=1, source_target_pairs={{32,0},{64,32},{96,64},{128,96},{160,128},{192,160},{224,192},{256... | collective-permute-start | bytes 786440 | tf_op jit(solution)/shard_map/ppermute | solution.py:15
  14.4 5.8 %collective-permute-start.4 = (bf16[2048,64]{0,1:T(8,128)(2,1)S(1)}, bf16[2048,64]{0,1:T(8,128)(2,1)}, u32[]{:S(2)}, u32[]{:S(2)}) collective-permute-start(bf16[2048,64]{0,1:T(8,128)(2,1)S(1)} %get-tuple-element.21), channel_id=1, source_target_pairs={{1,0},{2,1},{3,2},{4,3},{5,4},{6,5},{7,6},{8,7},{9,8},{10,9},{11,1... | collective-permute-start | bytes 786440 | tf_op jit(solution)/shard_map/ppermute | solution.py:15
  38.5 2.5 %fusion.36 = bf16[2048,256]{1,0:T(8,128)(2,1)} fusion(bf16[2048,64]{0,1:T(8,128)(2,1)} %collective-permute-done, f32[256]{0:T(256)S(1)} %bitcast.133, bf16[1,1,64,256]{3,2,1,0:T(8,128)(2,1)S(1)} %copy-done), kind=kOutput, calls=%fused_computation.56 | convolution fusion | flops 68681728 | bytes 1344512 | tf_op jit(solution)/shard_map/dot_general | solution.py:33
  41.0 3.0 %fusion.21 = bf16[2048,256]{1,0:T(8,128)(2,1)} fusion(bf16[2048,256]{1,0:T(8,128)(2,1)} %fusion.36, f32[256]{0:T(256)S(1)} %bitcast.125, f32[256]{0:T(256)S(1)} %bitcast.129, bf16[1,1,4,256,256]{4,3,2,1,0:T(8,128)(2,1)S(1)} %copy-done.10), kind=kOutput, calls=%fused_computation.41 | convolution fusion | flops 540016640 | bytes 2361344 | tf_op jit(solution)/shard_map/dot_general | solution.py:37
  51.2 3.0 %fusion.25 = bf16[2048,256]{1,0:T(8,128)(2,1)} fusion(bf16[2048,256]{1,0:T(8,128)(2,1)} %fusion.37, f32[256]{0:T(256)S(1)} %bitcast.126, f32[256]{0:T(256)S(1)} %bitcast.130, bf16[1,1,4,256,256]{4,3,2,1,0:T(8,128)(2,1)S(1)} %copy-done.11), kind=kOutput, calls=%fused_computation.45 | convolution fusion | flops 540016640 | bytes 2361344 | tf_op jit(solution)/shard_map/dot_general | solution.py:37
  56.7 10.1 %collective-permute-start.3 = (f32[2048]{0:T(1024)S(1)}, f32[2048]{0:T(1024)S(1)}, u32[]{:S(2)}, u32[]{:S(2)}) collective-permute-start(f32[2048]{0:T(1024)S(1)} %compare_select_fusion.2), channel_id=1, source_target_pairs={{32,0},{64,32},{96,64},{128,96},{160,128},{192,160},{224,192},{256... | collective-permute-start | bytes 24584 | tf_op jit(solution)/shard_map/ppermute | solution.py:15
  69.2 3.1 %fusion.33 = bf16[2048,256]{1,0:T(8,128)(2,1)} fusion(bf16[2048,256]{1,0:T(8,128)(2,1)} %fusion.39, f32[256]{0:T(256)S(1)} %bitcast.127, f32[256]{0:T(256)S(1)} %bitcast.131, bf16[1,1,4,256,256]{4,3,2,1,0:T(8,128)(2,1)S(1)} %copy-done.12), kind=kOutput, calls=%fused_computation.53 | convolution fusion | flops 540016640 | bytes 2361344 | tf_op jit(solution)/shard_map/dot_general | solution.py:37
  82.4 2.6 %collective-permute-start.5 = (f32[2048]{0:T(1024)S(1)}, f32[2048]{0:T(1024)S(1)}, u32[]{:S(2)}, u32[]{:S(2)}) collective-permute-start(f32[2048]{0:T(1024)S(1)} %compare_select_fusion.1), channel_id=1, source_target_pairs={{0,1},{1,2},{2,3},{3,4},{4,5},{5,6},{6,7},{7,8},{8,9},{9,10},{10,1... | collective-permute-start | bytes 24584 | tf_op jit(solution)/shard_map/ppermute | solution.py:15
  96.2 3.9 %collective-permute-start.8 = (f32[1,32,128]{2,1,0:T(8,128)S(1)}, f32[1,32,128]{2,1,0:T(8,128)S(1)}, u32[]{:S(2)}, u32[]{:S(2)}) collective-permute-start(f32[1,32,128]{2,1,0:T(8,128)S(1)} %get-tuple-element.37), channel_id=1, source_target_pairs={{32,0},{64,32},{96,64},{128,96},{160,128},{192,160},{224,192},{256... | collective-permute-start | bytes 49160 | tf_op jit(solution)/shard_map/ppermute | solution.py:26
  102.1 9.9 %collective-permute-done.9 = f32[1,32,128]{2,1,0:T(8,128)S(1)} collective-permute-done((f32[1,32,128]{2,1,0:T(8,128)S(1)}, f32[1,32,128]{2,1,0:T(8,128)S(1)}, u32[]{:S(2)}, u32[]{:S(2)}) %collective-permute-start.9) | collective-permute-done | bytes 16416 | tf_op jit(solution)/shard_map/ppermute | solution.py:25
  112.0 3.8 %collective-permute-start.10 = (f32[34,1,128]{2,1,0:T(1,128)S(1)}, f32[34,1,128]{2,1,0:T(1,128)S(1)}, u32[]{:S(2)}, u32[]{:S(2)}) collective-permute-start(f32[34,1,128]{2,1,0:T(1,128)S(1)} %get-tuple-element.28), channel_id=1, source_target_pairs={{1,0},{2,1},{3,2},{4,3},{5,4},{6,5},{7,6},{8,7},{9,8},{10,9},{11,1... | collective-permute-start | bytes 52232 | tf_op jit(solution)/shard_map/ppermute | solution.py:26
  117.8 5.2 %collective-permute-done.11 = f32[34,1,128]{2,1,0:T(1,128)S(1)} collective-permute-done((f32[34,1,128]{2,1,0:T(1,128)S(1)}, f32[34,1,128]{2,1,0:T(1,128)S(1)}, u32[]{:S(2)}, u32[]{:S(2)}) %collective-permute-start.11) | collective-permute-done | bytes 17440 | tf_op jit(solution)/shard_map/ppermute | solution.py:25
  125.1 3.9 %collective-permute-start.13 = (f32[1,32,128]{2,1,0:T(8,128)S(1)}, f32[1,32,128]{2,1,0:T(8,128)S(1)}, u32[]{:S(2)}, u32[]{:S(2)}) collective-permute-start(f32[1,32,128]{2,1,0:T(8,128)S(1)} %get-tuple-element.34), channel_id=1, source_target_pairs={{0,32},{32,64},{64,96},{96,128},{128,160},{160,192},{192,224},{224... | collective-permute-start | bytes 49160 | tf_op jit(solution)/shard_map/ppermute | solution.py:25
  129.1 7.7 %collective-permute-done.13 = f32[1,32,128]{2,1,0:T(8,128)S(1)} collective-permute-done((f32[1,32,128]{2,1,0:T(8,128)S(1)}, f32[1,32,128]{2,1,0:T(8,128)S(1)}, u32[]{:S(2)}, u32[]{:S(2)}) %collective-permute-start.13) | collective-permute-done | bytes 16416 | tf_op jit(solution)/shard_map/ppermute | solution.py:25
  138.8 2.4 %collective-permute-start.15 = (f32[34,1,128]{2,1,0:T(1,128)S(1)}, f32[34,1,128]{2,1,0:T(1,128)S(1)}, u32[]{:S(2)}, u32[]{:S(2)}) collective-permute-start(f32[34,1,128]{2,1,0:T(1,128)S(1)} %get-tuple-element.27), channel_id=1, source_target_pairs={{0,1},{1,2},{2,3},{3,4},{4,5},{5,6},{6,7},{7,8},{8,9},{9,10},{10,1... | collective-permute-start | bytes 52232 | tf_op jit(solution)/shard_map/ppermute | solution.py:25
  141.2 4.8 %collective-permute-done.15 = f32[34,1,128]{2,1,0:T(1,128)S(1)} collective-permute-done((f32[34,1,128]{2,1,0:T(1,128)S(1)}, f32[34,1,128]{2,1,0:T(1,128)S(1)}, u32[]{:S(2)}, u32[]{:S(2)}) %collective-permute-start.15) | collective-permute-done | bytes 17440 | tf_op jit(solution)/shard_map/ppermute | solution.py:25
  148.1 3.9 %collective-permute-start.17 = (f32[1,32,128]{2,1,0:T(8,128)S(1)}, f32[1,32,128]{2,1,0:T(8,128)S(1)}, u32[]{:S(2)}, u32[]{:S(2)}) collective-permute-start(f32[1,32,128]{2,1,0:T(8,128)S(1)} %get-tuple-element.32), channel_id=1, source_target_pairs={{0,32},{32,64},{64,96},{96,128},{128,160},{160,192},{192,224},{224... | collective-permute-start | bytes 49160 | tf_op jit(solution)/shard_map/ppermute | solution.py:25
  152.0 7.7 %collective-permute-done.17 = f32[1,32,128]{2,1,0:T(8,128)S(1)} collective-permute-done((f32[1,32,128]{2,1,0:T(8,128)S(1)}, f32[1,32,128]{2,1,0:T(8,128)S(1)}, u32[]{:S(2)}, u32[]{:S(2)}) %collective-permute-start.17) | collective-permute-done | bytes 16416 | tf_op jit(solution)/shard_map/ppermute | solution.py:25
  161.7 2.4 %collective-permute-start.19 = (f32[34,1,128]{2,1,0:T(1,128)S(1)}, f32[34,1,128]{2,1,0:T(1,128)S(1)}, u32[]{:S(2)}, u32[]{:S(2)}) collective-permute-start(f32[34,1,128]{2,1,0:T(1,128)S(1)} %get-tuple-element.25), channel_id=1, source_target_pairs={{0,1},{1,2},{2,3},{3,4},{4,5},{5,6},{6,7},{7,8},{8,9},{9,10},{10,1... | collective-permute-start | bytes 52232 | tf_op jit(solution)/shard_map/ppermute | solution.py:25
  164.1 4.8 %collective-permute-done.19 = f32[34,1,128]{2,1,0:T(1,128)S(1)} collective-permute-done((f32[34,1,128]{2,1,0:T(1,128)S(1)}, f32[34,1,128]{2,1,0:T(1,128)S(1)}, u32[]{:S(2)}, u32[]{:S(2)}) %collective-permute-start.19) | collective-permute-done | bytes 17440 | tf_op jit(solution)/shard_map/ppermute | solution.py:25
  171.0 3.9 %collective-permute-start.21 = (f32[1,32,128]{2,1,0:T(8,128)S(1)}, f32[1,32,128]{2,1,0:T(8,128)S(1)}, u32[]{:S(2)}, u32[]{:S(2)}) collective-permute-start(f32[1,32,128]{2,1,0:T(8,128)S(1)} %get-tuple-element.31), channel_id=1, source_target_pairs={{0,32},{32,64},{64,96},{96,128},{128,160},{160,192},{192,224},{224... | collective-permute-start | bytes 49160 | tf_op jit(solution)/shard_map/ppermute | solution.py:25
  174.9 7.7 %collective-permute-done.21 = f32[1,32,128]{2,1,0:T(8,128)S(1)} collective-permute-done((f32[1,32,128]{2,1,0:T(8,128)S(1)}, f32[1,32,128]{2,1,0:T(8,128)S(1)}, u32[]{:S(2)}, u32[]{:S(2)}) %collective-permute-start.21) | collective-permute-done | bytes 16416 | tf_op jit(solution)/shard_map/ppermute | solution.py:25
  184.6 2.4 %collective-permute-start.23 = (f32[34,1,128]{2,1,0:T(1,128)S(1)}, f32[34,1,128]{2,1,0:T(1,128)S(1)}, u32[]{:S(2)}, u32[]{:S(2)}) collective-permute-start(f32[34,1,128]{2,1,0:T(1,128)S(1)} %get-tuple-element.23), channel_id=1, source_target_pairs={{0,1},{1,2},{2,3},{3,4},{4,5},{5,6},{6,7},{7,8},{8,9},{9,10},{10,1... | collective-permute-start | bytes 52232 | tf_op jit(solution)/shard_map/ppermute | solution.py:25
  187.0 4.8 %collective-permute-done.23 = f32[34,1,128]{2,1,0:T(1,128)S(1)} collective-permute-done((f32[34,1,128]{2,1,0:T(1,128)S(1)}, f32[34,1,128]{2,1,0:T(1,128)S(1)}, u32[]{:S(2)}, u32[]{:S(2)}) %collective-permute-start.23) | collective-permute-done | bytes 17440 | tf_op jit(solution)/shard_map/ppermute | solution.py:25
  (153 shorter events, 75.1 us)
Async XLA Ops:
  2.7 35.8 %collective-permute-start = (bf16[2048,64]{0,1:T(8,128)(2,1)}, bf16[2048,64]{0,1:T(8,128)(2,1)}, u32[]{:S(2)}, u32[]{:S(2)}) collective-permute-start(bf16[2048,64]{0,1:T(8,128)(2,1)} %get-tuple-element.18), channel_id=1, source_target_pairs={{32,0},{64,32},{96,64},{128,96},{160,128},{192,160},{224,192},{256... | collective-permute-start | bytes 786440 | tf_op jit(solution)/shard_map/ppermute | solution.py:15
  10.6 38.2 %collective-permute-start.2 = (bf16[2048,64]{0,1:T(8,128)(2,1)S(1)}, bf16[2048,64]{0,1:T(8,128)(2,1)}, u32[]{:S(2)}, u32[]{:S(2)}) collective-permute-start(bf16[2048,64]{0,1:T(8,128)(2,1)S(1)} %get-tuple-element.19), channel_id=1, source_target_pairs={{0,32},{32,64},{64,96},{96,128},{128,160},{160,192},{192,224},{224... | collective-permute-start | bytes 786440 | tf_op jit(solution)/shard_map/ppermute | solution.py:15
  12.5 54.3 %collective-permute-start.6 = (bf16[2048,64]{0,1:T(8,128)(2,1)S(1)}, bf16[2048,64]{0,1:T(8,128)(2,1)}, u32[]{:S(2)}, u32[]{:S(2)}) collective-permute-start(bf16[2048,64]{0,1:T(8,128)(2,1)S(1)} %get-tuple-element.20), channel_id=1, source_target_pairs={{0,1},{1,2},{2,3},{3,4},{4,5},{5,6},{6,7},{7,8},{8,9},{9,10},{10,1... | collective-permute-start | bytes 786440 | tf_op jit(solution)/shard_map/ppermute | solution.py:15
  14.4 62.3 %collective-permute-start.4 = (bf16[2048,64]{0,1:T(8,128)(2,1)S(1)}, bf16[2048,64]{0,1:T(8,128)(2,1)}, u32[]{:S(2)}, u32[]{:S(2)}) collective-permute-start(bf16[2048,64]{0,1:T(8,128)(2,1)S(1)} %get-tuple-element.21), channel_id=1, source_target_pairs={{1,0},{2,1},{3,2},{4,3},{5,4},{6,5},{7,6},{8,7},{9,8},{10,9},{11,1... | collective-permute-start | bytes 786440 | tf_op jit(solution)/shard_map/ppermute | solution.py:15
  46.5 38.5 %collective-permute-start.1 = (f32[2048]{0:T(1024)S(1)}, f32[2048]{0:T(1024)S(1)}, u32[]{:S(2)}, u32[]{:S(2)}) collective-permute-start(f32[2048]{0:T(1024)S(1)} %compare_select_fusion.3), channel_id=1, source_target_pairs={{0,32},{32,64},{64,96},{96,128},{128,160},{160,192},{192,224},{224... | collective-permute-start | bytes 24584 | tf_op jit(solution)/shard_map/ppermute | solution.py:15
  56.7 29.0 %collective-permute-start.3 = (f32[2048]{0:T(1024)S(1)}, f32[2048]{0:T(1024)S(1)}, u32[]{:S(2)}, u32[]{:S(2)}) collective-permute-start(f32[2048]{0:T(1024)S(1)} %compare_select_fusion.2), channel_id=1, source_target_pairs={{32,0},{64,32},{96,64},{128,96},{160,128},{192,160},{224,192},{256... | collective-permute-start | bytes 24584 | tf_op jit(solution)/shard_map/ppermute | solution.py:15
  74.8 11.6 %collective-permute-start.7 = (f32[2048]{0:T(1024)S(1)}, f32[2048]{0:T(1024)S(1)}, u32[]{:S(2)}, u32[]{:S(2)}) collective-permute-start(f32[2048]{0:T(1024)S(1)} %compare_select_fusion), channel_id=1, source_target_pairs={{1,0},{2,1},{3,2},{4,3},{5,4},{6,5},{7,6},{8,7},{9,8},{10,9},{11,1... | collective-permute-start | bytes 24584 | tf_op jit(solution)/shard_map/ppermute | solution.py:15
  82.4 8.7 %collective-permute-start.5 = (f32[2048]{0:T(1024)S(1)}, f32[2048]{0:T(1024)S(1)}, u32[]{:S(2)}, u32[]{:S(2)}) collective-permute-start(f32[2048]{0:T(1024)S(1)} %compare_select_fusion.1), channel_id=1, source_target_pairs={{0,1},{1,2},{2,3},{3,4},{4,5},{5,6},{6,7},{7,8},{8,9},{9,10},{10,1... | collective-permute-start | bytes 24584 | tf_op jit(solution)/shard_map/ppermute | solution.py:15
  96.2 5.9 %collective-permute-start.8 = (f32[1,32,128]{2,1,0:T(8,128)S(1)}, f32[1,32,128]{2,1,0:T(8,128)S(1)}, u32[]{:S(2)}, u32[]{:S(2)}) collective-permute-start(f32[1,32,128]{2,1,0:T(8,128)S(1)} %get-tuple-element.37), channel_id=1, source_target_pairs={{32,0},{64,32},{96,64},{128,96},{160,128},{192,160},{224,192},{256... | collective-permute-start | bytes 49160 | tf_op jit(solution)/shard_map/ppermute | solution.py:26
  100.1 11.8 %collective-permute-start.9 = (f32[1,32,128]{2,1,0:T(8,128)S(1)}, f32[1,32,128]{2,1,0:T(8,128)S(1)}, u32[]{:S(2)}, u32[]{:S(2)}) collective-permute-start(f32[1,32,128]{2,1,0:T(8,128)S(1)} %get-tuple-element.36), channel_id=1, source_target_pairs={{0,32},{32,64},{64,96},{96,128},{128,160},{160,192},{192,224},{224... | collective-permute-start | bytes 49160 | tf_op jit(solution)/shard_map/ppermute | solution.py:25
  112.0 5.8 %collective-permute-start.10 = (f32[34,1,128]{2,1,0:T(1,128)S(1)}, f32[34,1,128]{2,1,0:T(1,128)S(1)}, u32[]{:S(2)}, u32[]{:S(2)}) collective-permute-start(f32[34,1,128]{2,1,0:T(1,128)S(1)} %get-tuple-element.28), channel_id=1, source_target_pairs={{1,0},{2,1},{3,2},{4,3},{5,4},{6,5},{7,6},{8,7},{9,8},{10,9},{11,1... | collective-permute-start | bytes 52232 | tf_op jit(solution)/shard_map/ppermute | solution.py:26
  115.8 7.2 %collective-permute-start.11 = (f32[34,1,128]{2,1,0:T(1,128)S(1)}, f32[34,1,128]{2,1,0:T(1,128)S(1)}, u32[]{:S(2)}, u32[]{:S(2)}) collective-permute-start(f32[34,1,128]{2,1,0:T(1,128)S(1)} %get-tuple-element.29), channel_id=1, source_target_pairs={{0,1},{1,2},{2,3},{3,4},{4,5},{5,6},{6,7},{7,8},{8,9},{9,10},{10,1... | collective-permute-start | bytes 52232 | tf_op jit(solution)/shard_map/ppermute | solution.py:25
  123.2 5.9 %collective-permute-start.12 = (f32[1,32,128]{2,1,0:T(8,128)S(1)}, f32[1,32,128]{2,1,0:T(8,128)S(1)}, u32[]{:S(2)}, u32[]{:S(2)}) collective-permute-start(f32[1,32,128]{2,1,0:T(8,128)S(1)} %get-tuple-element.35), channel_id=1, source_target_pairs={{32,0},{64,32},{96,64},{128,96},{160,128},{192,160},{224,192},{256... | collective-permute-start | bytes 49160 | tf_op jit(solution)/shard_map/ppermute | solution.py:26
  125.1 11.7 %collective-permute-start.13 = (f32[1,32,128]{2,1,0:T(8,128)S(1)}, f32[1,32,128]{2,1,0:T(8,128)S(1)}, u32[]{:S(2)}, u32[]{:S(2)}) collective-permute-start(f32[1,32,128]{2,1,0:T(8,128)S(1)} %get-tuple-element.34), channel_id=1, source_target_pairs={{0,32},{32,64},{64,96},{96,128},{128,160},{160,192},{192,224},{224... | collective-permute-start | bytes 49160 | tf_op jit(solution)/shard_map/ppermute | solution.py:25
  136.8 4.3 %collective-permute-start.14 = (f32[34,1,128]{2,1,0:T(1,128)S(1)}, f32[34,1,128]{2,1,0:T(1,128)S(1)}, u32[]{:S(2)}, u32[]{:S(2)}) collective-permute-start(f32[34,1,128]{2,1,0:T(1,128)S(1)} %get-tuple-element.26), channel_id=1, source_target_pairs={{1,0},{2,1},{3,2},{4,3},{5,4},{6,5},{7,6},{8,7},{9,8},{10,9},{11,1... | collective-permute-start | bytes 52232 | tf_op jit(solution)/shard_map/ppermute | solution.py:26
  138.8 7.2 %collective-permute-start.15 = (f32[34,1,128]{2,1,0:T(1,128)S(1)}, f32[34,1,128]{2,1,0:T(1,128)S(1)}, u32[]{:S(2)}, u32[]{:S(2)}) collective-permute-start(f32[34,1,128]{2,1,0:T(1,128)S(1)} %get-tuple-element.27), channel_id=1, source_target_pairs={{0,1},{1,2},{2,3},{3,4},{4,5},{5,6},{6,7},{7,8},{8,9},{9,10},{10,1... | collective-permute-start | bytes 52232 | tf_op jit(solution)/shard_map/ppermute | solution.py:25
  146.1 5.9 %collective-permute-start.16 = (f32[1,32,128]{2,1,0:T(8,128)S(1)}, f32[1,32,128]{2,1,0:T(8,128)S(1)}, u32[]{:S(2)}, u32[]{:S(2)}) collective-permute-start(f32[1,32,128]{2,1,0:T(8,128)S(1)} %get-tuple-element.33), channel_id=1, source_target_pairs={{32,0},{64,32},{96,64},{128,96},{160,128},{192,160},{224,192},{256... | collective-permute-start | bytes 49160 | tf_op jit(solution)/shard_map/ppermute | solution.py:26
  148.1 11.6 %collective-permute-start.17 = (f32[1,32,128]{2,1,0:T(8,128)S(1)}, f32[1,32,128]{2,1,0:T(8,128)S(1)}, u32[]{:S(2)}, u32[]{:S(2)}) collective-permute-start(f32[1,32,128]{2,1,0:T(8,128)S(1)} %get-tuple-element.32), channel_id=1, source_target_pairs={{0,32},{32,64},{64,96},{96,128},{128,160},{160,192},{192,224},{224... | collective-permute-start | bytes 49160 | tf_op jit(solution)/shard_map/ppermute | solution.py:25
  159.8 4.3 %collective-permute-start.18 = (f32[34,1,128]{2,1,0:T(1,128)S(1)}, f32[34,1,128]{2,1,0:T(1,128)S(1)}, u32[]{:S(2)}, u32[]{:S(2)}) collective-permute-start(f32[34,1,128]{2,1,0:T(1,128)S(1)} %get-tuple-element.24), channel_id=1, source_target_pairs={{1,0},{2,1},{3,2},{4,3},{5,4},{6,5},{7,6},{8,7},{9,8},{10,9},{11,1... | collective-permute-start | bytes 52232 | tf_op jit(solution)/shard_map/ppermute | solution.py:26
  161.7 7.2 %collective-permute-start.19 = (f32[34,1,128]{2,1,0:T(1,128)S(1)}, f32[34,1,128]{2,1,0:T(1,128)S(1)}, u32[]{:S(2)}, u32[]{:S(2)}) collective-permute-start(f32[34,1,128]{2,1,0:T(1,128)S(1)} %get-tuple-element.25), channel_id=1, source_target_pairs={{0,1},{1,2},{2,3},{3,4},{4,5},{5,6},{6,7},{7,8},{8,9},{9,10},{10,1... | collective-permute-start | bytes 52232 | tf_op jit(solution)/shard_map/ppermute | solution.py:25
  169.1 5.9 %collective-permute-start.20 = (f32[1,32,128]{2,1,0:T(8,128)S(1)}, f32[1,32,128]{2,1,0:T(8,128)S(1)}, u32[]{:S(2)}, u32[]{:S(2)}) collective-permute-start(f32[1,32,128]{2,1,0:T(8,128)S(1)} %get-tuple-element.30), channel_id=1, source_target_pairs={{32,0},{64,32},{96,64},{128,96},{160,128},{192,160},{224,192},{256... | collective-permute-start | bytes 49160 | tf_op jit(solution)/shard_map/ppermute | solution.py:26
  171.0 11.6 %collective-permute-start.21 = (f32[1,32,128]{2,1,0:T(8,128)S(1)}, f32[1,32,128]{2,1,0:T(8,128)S(1)}, u32[]{:S(2)}, u32[]{:S(2)}) collective-permute-start(f32[1,32,128]{2,1,0:T(8,128)S(1)} %get-tuple-element.31), channel_id=1, source_target_pairs={{0,32},{32,64},{64,96},{96,128},{128,160},{160,192},{192,224},{224... | collective-permute-start | bytes 49160 | tf_op jit(solution)/shard_map/ppermute | solution.py:25
  182.7 4.3 %collective-permute-start.22 = (f32[34,1,128]{2,1,0:T(1,128)S(1)}, f32[34,1,128]{2,1,0:T(1,128)S(1)}, u32[]{:S(2)}, u32[]{:S(2)}) collective-permute-start(f32[34,1,128]{2,1,0:T(1,128)S(1)} %get-tuple-element.22), channel_id=1, source_target_pairs={{1,0},{2,1},{3,2},{4,3},{5,4},{6,5},{7,6},{8,7},{9,8},{10,9},{11,1... | collective-permute-start | bytes 52232 | tf_op jit(solution)/shard_map/ppermute | solution.py:26
  184.6 7.2 %collective-permute-start.23 = (f32[34,1,128]{2,1,0:T(1,128)S(1)}, f32[34,1,128]{2,1,0:T(1,128)S(1)}, u32[]{:S(2)}, u32[]{:S(2)}) collective-permute-start(f32[34,1,128]{2,1,0:T(1,128)S(1)} %get-tuple-element.23), channel_id=1, source_target_pairs={{0,1},{1,2},{2,3},{3,4},{4,5},{5,6},{6,7},{7,8},{8,9},{9,10},{10,1... | collective-permute-start | bytes 52232 | tf_op jit(solution)/shard_map/ppermute | solution.py:25
  (14 other events, 131.5 us)
where the time goes:
time: 195 us; the launch traced here: 194 us
  starting transfers between devices  76.5 us (39%)
  waiting for transfers between devices  52.6 us (27%)
  matrix products  29.4 us (15%)
  local copies, waits for them, and re-layouts  24.1 us (12%)
  other arithmetic  9.73 us (5%)
    ppermute x8, waiting for transfers between devices, extended(): before = lax.ppermute(last, axis, up)  52.5 us
    ppermute x8, starting transfers between devices, shifted(): return lax.ppermute(shard, axis, pairs)  34.3 us
    ppermute x8, starting transfers between devices, extended(): before = lax.ppermute(last, axis, up)  22.8 us
    ppermute x8, starting transfers between devices, extended(): after = lax.ppermute(leading, axis, down)  19.3 us
    dot_general x8, matrix products, network(): jnp.dot(hidden, w_hid[levels], preferred_element_type=jnp.float32)  19.3 us
    broadcast_in_dim x20, local copies, waits for them, and re-layouts, band_spread(): band = jnp.where(hits, values[:, None], 0.0).reshape(band_shape)  11.7 us
    dot_general x4, matrix products, network(): jnp.dot(features, w_in, preferred_element_type=jnp.float32) + biases[0]  8.66 us
    eq x10, local copies, waits for them, and re-layouts, band_spread(): hits = within[:, None] == jnp.arange(slot, dtype=jnp.int32)[None, :]  4.73 us
  transfers between devices with their start and end apart: 24, of which 8 were waited for; matrix products, arithmetic and copies ran while one was open for 28% of the time, Pallas kernels for 0%

commit v1 on v0

v1 whole, which is shorter than its diff:
```python
import functools

import jax
import jax.numpy as jnp
from jax import lax
from jax.experimental import pallas as pl
from jax.experimental.pallas import tpu as pltpu
from jax.sharding import PartitionSpec as P

MESH = pl.DeviceIdType.MESH
F32, BF16, I32 = jnp.float32, jnp.bfloat16, jnp.int32
HX, HY = 4, 8
AROUND = ((-1, 0), (1, 0), (0, -1), (0, 1), (-1, -1), (-1, 1), (1, -1), (1, 1))


def spread(row, index):
    wide = jnp.broadcast_to(row, index.shape)
    return jnp.take_along_axis(wide, index, axis=1, mode="promise_in_bounds")


def blend_kernel(
    dens, feat, cell, count, w_in, w_hid, w_out, bias, out,
    ext, recv, values, back, cells, coef_x, coef_y, win_t, whid_t, bias_w,
    feat_send, feat_recv, back_send, back_recv, halo_send, halo_recv, out_sem,
):
    ix, iy = lax.axis_index("bx"), lax.axis_index("by")
    nx, ny = lax.axis_size("bx"), lax.axis_size("by")
    size_x, size_y, size_z = dens.shape
    listed = cell.shape[1]
    rows = listed // 128

    def there(dx, dy):
        ok_x = jnp.bool_(True) if dx == 0 else (ix + dx >= 0 if dx < 0 else ix + dx < nx)
        ok_y = jnp.bool_(True) if dy == 0 else (iy + dy >= 0 if dy < 0 else iy + dy < ny)
        return ok_x & ok_y

    def at(dx, dy):
        return {"bx": ix + dx, "by": iy + dy}

    ext[...] = jnp.zeros_like(ext)
    back[...] = jnp.zeros_like(back)
    barrier = pltpu.get_barrier_semaphore()
    for dx, dy in AROUND:
        @pl.when(there(dx, dy))
        def _(dx=dx, dy=dy):
            pl.semaphore_signal(barrier, inc=1, device_id=at(dx, dy), device_id_type=MESH)

    for layer in range(w_hid.shape[0]):
        whid_t[layer] = w_hid[layer].T
    win_t[...] = w_in[...].T
    for layer in range(bias.shape[0]):
        column = jnp.broadcast_to(bias[layer : layer + 1, :], (128, bias.shape[1])).T
        bias_w[layer] = column
    ranks = lax.broadcasted_iota(I32, (1, listed), 1)
    for s in range(4):
        usable = (ranks < count[s]) & there(*AROUND[s])
        height = jnp.where(usable, cell[s : s + 1, :] & (size_z - 1), -1)
        for r in range(rows):
            cells[s * rows + r : s * rows + r + 1, :] = height[:, r * 128 : (r + 1) * 128]

    lane = lax.broadcasted_iota(I32, (8, 128), 1)
    sub = lax.broadcasted_iota(I32, (8, 128), 0)
    groups = size_y // 8
    index = [4 * (8 * g + sub) + lane // 32 for g in range(groups)]
    dist_y = [((8 * g + sub).astype(F32) + 0.5) / size_y - 0.5 for g in range(groups)]

    def list_rows(table, x, pair, parity):
        row_x = table[pl.ds(x, 1), :]
        row_2 = table[pl.ds(2 * rows + pair, 1), :]
        row_3 = table[pl.ds(3 * rows + pair, 1), :]
        along_x = [spread(row_x, index[g]) for g in range(groups)]
        half = groups // 2
        along_y = [spread(row_2 if g < half else row_3, index[g % half + half * parity]) for g in range(groups)]
        return along_x, along_y

    def prepare(pair, _):
        for parity in range(2):
            x = 2 * pair + parity
            dist_x = (x.astype(F32) + 0.5) / size_x - 0.5
            off_x = jnp.where(x < size_x // 2, -1.0, 1.0)
            along_x, along_y = list_rows(cells, x, pair, parity)
            for g in range(groups):
                off_y = -1.0 if g < groups // 2 else 1.0
                sq_x, sq_y = dist_x * dist_x, dist_y[g] * dist_y[g]
                far_x, far_y = dist_x - off_x, dist_y[g] - off_y
                own = 1.0 / (sq_x + sq_y + 0.25)
                w_x = jnp.where(along_x[g] == lane, 1.0 / (far_x * far_x + sq_y + 0.25), 0.0)
                w_y = jnp.where(along_y[g] == lane, 1.0 / (sq_x + far_y * far_y + 0.25), 0.0)
                share = 1.0 / (own + w_x + w_y)
                voxels = pl.ds(8 * g, 8)
                ext[HX + x, pl.ds(HY + 8 * g, 8), :] = own * dens[x, voxels, :] * share
                coef_x[x, voxels, :] = w_x * share
                coef_y[x, voxels, :] = w_y * share
        return 0

    lax.fori_loop(0, size_x // 2, prepare, 0)

    pl.semaphore_wait(barrier, sum(there(dx, dy).astype(I32) for dx, dy in AROUND))

    def opposite(s):
        dx = jnp.where(s == 0, 1, jnp.where(s == 1, -1, 0))
        dy = jnp.where(s == 2, 1, jnp.where(s == 3, -1, 0))
        ok = (ix + dx >= 0) & (ix + dx < nx) & (iy + dy >= 0) & (iy + dy < ny)
        return ok, dx, dy

    def feature_copy(s, dx, dy):
        return pltpu.make_async_remote_copy(
            src_ref=feat.at[s], dst_ref=recv.at[s], send_sem=feat_send.at[s], recv_sem=feat_recv.at[s],
            device_id=at(dx, dy), device_id_type=MESH)

    for s in range(4):
        @pl.when(there(*AROUND[s]))
        def _(s=s):
            feature_copy(s, *AROUND[s]).start()

    def value_copy(s, dx, dy):
        return pltpu.make_async_remote_copy(
            src_ref=values.at[s], dst_ref=back.at[s], send_sem=back_send.at[s], recv_sem=back_recv.at[s],
            device_id=at(dx, dy), device_id_type=MESH)

    head = jnp.broadcast_to(w_out[...].astype(F32), (16, w_out.shape[1])).astype(BF16)
    last = ix % 4 == 3

    def evaluate(step, _):
        s = jnp.where(step < 2, step + 2, jnp.where(last, 3 - step, step - 2))
        ok, dx, dy = opposite(s)

        @pl.when(ok)
        def _():
            feature_copy(s, dx, dy).wait_recv()

            def layer(weights, hidden, level):
                wide = jnp.concatenate([bias_w[level]] * (listed // 128), axis=1)
                total = jnp.dot(weights, hidden, preferred_element_type=F32) + wide
                return jnp.maximum(total.astype(BF16), 0)

            hidden = layer(win_t[...], recv[s], 0)
            for level in range(whid_t.shape[0]):
                hidden = layer(whid_t[level], hidden, level + 1)
            raw = jnp.dot(head, hidden, preferred_element_type=F32)[0:1, :]
            result = jnp.maximum(raw, 0.0) + jnp.log1p(jnp.exp(-jnp.abs(raw)))
            for r in range(rows):
                values[s, r : r + 1, :] = result[:, r * 128 : (r + 1) * 128]
            value_copy(s, dx, dy).start()

        return 0

    lax.fori_loop(0, 4, evaluate, 0)

    for s in range(4):
        @pl.when(there(*AROUND[s]))
        def _(s=s):
            value_copy(s, *AROUND[s]).wait_recv()

    def blend(pair, _):
        for parity in range(2):
            x = 2 * pair + parity
            side_x = pair // (rows // 2)
            row_x = back[side_x, pl.ds(x - side_x * rows, 1), :]
            row_2 = back[2, pl.ds(pair, 1), :]
            row_3 = back[3, pl.ds(pair, 1), :]
            half = groups // 2
            for g in range(groups):
                voxels = pl.ds(8 * g, 8)
                at_x = spread(row_x, index[g])
                at_y = spread(row_2 if g < half else row_3, index[g % half + half * parity])
                place = pl.ds(HY + 8 * g, 8)
                ext[HX + x, place, :] = (
                    ext[HX + x, place, :] + coef_x[x, voxels, :] * at_x + coef_y[x, voxels, :] * at_y
                )
        return 0

    lax.fori_loop(0, size_x // 2, blend, 0)

    def halo_copy(n, dx, dy):
        def cut(d, own, width, inner):
            if d == 0:
                return pl.ds(own, inner), pl.ds(own, inner)
            if d > 0:
                return pl.ds(own + inner - width, width), pl.ds(own - width, width)
            return pl.ds(own, width), pl.ds(own + inner, width)

        src_x, dst_x = cut(dx, HX, HX, size_x)
        src_y, dst_y = cut(dy, HY, HY, size_y)
        return pltpu.make_async_remote_copy(
            src_ref=ext.at[src_x, src_y, :], dst_ref=ext.at[dst_x, dst_y, :],
            send_sem=halo_send.at[n], recv_sem=halo_recv.at[n],
            device_id=at(dx, dy), device_id_type=MESH)

    for n, (dx, dy) in enumerate(AROUND):
        @pl.when(there(dx, dy))
        def _(n=n, dx=dx, dy=dy):
            halo_copy(n, dx, dy).start()

    for s in range(4):
        @pl.when(there(*AROUND[s]))
        def _(s=s):
            feature_copy(s, *AROUND[s]).wait_send()

        @pl.when(there(-AROUND[s][0], -AROUND[s][1]))
        def _(s=s):
            value_copy(s, -AROUND[s][0], -AROUND[s][1]).wait_send()

    for n, (dx, dy) in enumerate(AROUND):
        @pl.when(there(-dx, -dy))
        def _(n=n, dx=dx, dy=dy):
            halo_copy(n, -dx, -dy).wait_recv()

        @pl.when(there(dx, dy))
        def _(n=n, dx=dx, dy=dy):
            halo_copy(n, dx, dy).wait_send()

    copy = pltpu.make_async_copy(ext, out, out_sem)
    copy.start()
    copy.wait()


def finish_kernel(ext, smoothed, normals, one, two):
    ix, iy = lax.axis_index("bx"), lax.axis_index("by")
    nx, ny = lax.axis_size("bx"), lax.axis_size("by")
    size_x, size_y, size_z = smoothed.shape
    full_x, full_y = size_x + 2 * HX, size_y + 2 * HY
    sub = lax.broadcasted_iota(I32, (full_y, size_z), 0)
    inside_y = ((sub >= HY) | (iy > 0)) & ((sub < HY + size_y) | (iy < ny - 1))
    keep_y = jnp.where(inside_y, 0.2, 0.0)

    def one_pass(src, dst, margin):
        def step(x, _):
            centre = src[x]
            total = (
                centre + src[x + 1] + src[x - 1]
                + pltpu.roll(centre, 1, 0) + pltpu.roll(centre, full_y - 1, 0)
            )
            inside = ((x >= HX) | (ix > 0)) & ((x < HX + size_x) | (ix < nx - 1))
            dst[x] = total * jnp.where(inside, keep_y, 0.0)
            return 0

        lax.fori_loop(margin, full_x - margin, step, 0, unroll=2)

    one_pass(ext, one, 1)
    one_pass(one, two, 2)
    one_pass(two, one, 3)
    last_z = lax.broadcasted_iota(I32, (size_y, size_z), 1)

    def gradient(x, _):
        row = HX + x
        centre = one[row]
        own = centre[HY : HY + size_y]
        grad_x = one[row + 1, HY : HY + size_y, :] - one[row - 1, HY : HY + size_y, :]
        grad_y = (pltpu.roll(centre, full_y - 1, 0) - pltpu.roll(centre, 1, 0))[HY : HY + size_y]
        after = jnp.where(last_z == size_z - 1, 0.0, pltpu.roll(own, size_z - 1, 1))
        before = jnp.where(last_z == 0, 0.0, pltpu.roll(own, 1, 1))
        grad_z = after - before
        factor = lax.rsqrt(1.0 + grad_x * grad_x + grad_y * grad_y + grad_z * grad_z)
        smoothed[x] = own
        normals[0, x] = grad_x * factor
        normals[1, x] = grad_y * factor
        normals[2, x] = grad_z * factor
        return 0

    lax.fori_loop(0, size_x, gradient, 0, unroll=2)


def shards(density, band_feat, band_cell, band_count, w_in, w_hid, w_out, biases):
    size_x, size_y, size_z = density.shape
    feat = jnp.swapaxes(band_feat[0, 0], 1, 2)
    sides, width, listed = feat.shape
    levels, hidden = w_hid.shape[2], w_hid.shape[3]
    rows = listed // 128
    full = (size_x + 2 * HX, size_y + 2 * HY, size_z)
    vmem = pl.BlockSpec(memory_space=pltpu.VMEM)
    dma = pltpu.SemaphoreType.DMA
    ext = pl.pallas_call(
        blend_kernel,
        out_shape=jax.ShapeDtypeStruct(full, F32),
        in_specs=[vmem, pl.BlockSpec(memory_space=pl.ANY), vmem, pl.BlockSpec(memory_space=pltpu.SMEM)] + [vmem] * 4,
        out_specs=pl.BlockSpec(memory_space=pl.ANY),
        scratch_shapes=[
            pltpu.VMEM(full, F32),
            pltpu.VMEM((sides, width, listed), BF16),
            pltpu.VMEM((sides, rows, 128), F32),
            pltpu.VMEM((sides, rows, 128), F32),
            pltpu.VMEM((sides * rows, 128), I32),
            pltpu.VMEM(density.shape, F32),
            pltpu.VMEM(density.shape, F32),
            pltpu.VMEM((hidden, width), BF16),
            pltpu.VMEM((levels, hidden, hidden), BF16),
            pltpu.VMEM((levels + 1, hidden, 128), F32),
            dma((sides,)), dma((sides,)), dma((sides,)), dma((sides,)), dma((8,)), dma((8,)), dma,
        ],
        compiler_params=pltpu.CompilerParams(
            collective_id=0, has_side_effects=True, vmem_limit_bytes=48 << 20
        ),
        name="blend",
    )(
        density, feat, band_cell[0, 0], band_count[0, 0], w_in[0, 0], w_hid[0, 0],
        w_out[0, 0][None, :], biases[0, 0],
    )
    return pl.pallas_call(
        finish_kernel,
        out_shape=(
            jax.ShapeDtypeStruct(density.shape, F32),
            jax.ShapeDtypeStruct((3,) + density.shape, F32),
        ),
        in_specs=[vmem],
        out_specs=(vmem, vmem),
        scratch_shapes=[pltpu.VMEM(full, F32), pltpu.VMEM(full, F32)],
        compiler_params=pltpu.CompilerParams(vmem_limit_bytes=32 << 20),
        name="finish",
    )(ext)


def solution(mesh):
    placed = (
        P("bx", "by", None),
        P("bx", "by", None, None, None),
        P("bx", "by", None, None),
        P("bx", "by", None),
        P("bx", "by", None, None),
        P("bx", "by", None, None, None),
        P("bx", "by", None),
        P("bx", "by", None, None),
    )
    return jax.shard_map(
        shards,
        mesh=mesh,
        in_specs=placed,
        out_specs=(P("bx", "by", None), P(None, "bx", "by", None)),
        check_vma=False,
    )
```

time: 195 us -> 74.8 us (0.38)
  the two profiles are of different devices: /device:TPU:416 before, /device:TPU:159 now
where the time goes in v1:
time: 74.8 us; the launch traced here: 74.4 us
  Pallas kernels  66.9 us (89%)
  local copies, waits for them, and re-layouts  6.85 us (9%)
    pallas_call x1, Pallas kernels, shards(): pl.pallas_call(blend_kernel, out_shape=jax.ShapeDtypeStruct(full, F32), i...  62.9 us
    unnamed x15, local copies, waits for them, and re-layouts  6.85 us
    pallas_call x1, Pallas kernels, shards(): pl.pallas_call(finish_kernel, out_shape=(jax.ShapeDtypeStruct(density.sha...  3.98 us

profile of v1, /device:TPU:159, one launch (start us, length us, event | category | flops | bytes accessed | tf_op | source)
XLA Modules:
  0.0 74.4 jit_solution(10826962387112800819)
XLA Ops:
  0.6 0.7 copy.12
  1.3 0.0 copy-start
  1.3 1.2 %copy-done = bf16[1,1,4,2048,64]{3,4,2,1,0:T(8,128)(2,1)S(1)} copy-done((bf16[1,1,4,2048,64]{3,4,2,1,0:T(8,128)(2,1)S(1)}, bf16[1,1,4,2048,64]{3,4,2,1,0:T(8,128)(2,1)}, u32[]{:S(2)}) %copy-start) | copy-done | bytes 1048600
  2.5 0.0 copy-start.1
  2.5 1.0 %copy-done.1 = f32[32,32,128]{2,1,0:T(8,128)S(1)} copy-done((f32[32,32,128]{2,1,0:T(8,128)S(1)}, f32[32,32,128]{2,1,0:T(8,128)}, u32[]{:S(2)}) %copy-start.1) | copy-done | bytes 524312
  3.6 0.0 copy-start.2
  3.6 1.0 %copy-done.2 = bf16[1,1,4,256,256]{4,3,2,1,0:T(8,128)(2,1)S(1)} copy-done((bf16[1,1,4,256,256]{4,3,2,1,0:T(8,128)(2,1)S(1)}, bf16[1,1,4,256,256]{4,3,2,1,0:T(8,128)(2,1)}, u32[]{:S(2)}) %copy-start.2) | copy-done | bytes 524312
  4.6 0.0 copy-start.3
  4.6 0.8 %copy-done.3 = s32[1,1,4,2048]{3,2,1,0:T(4,128)S(1)} copy-done((s32[1,1,4,2048]{3,2,1,0:T(4,128)S(1)}, s32[1,1,4,2048]{3,2,1,0:T(4,128)}, u32[]{:S(2)}) %copy-start.3) | copy-done | bytes 32792
  5.4 0.0 copy-start.4
  5.4 0.8 %copy-done.4 = bf16[1,1,64,256]{3,2,1,0:T(8,128)(2,1)S(1)} copy-done((bf16[1,1,64,256]{3,2,1,0:T(8,128)(2,1)S(1)}, bf16[1,1,64,256]{3,2,1,0:T(8,128)(2,1)}, u32[]{:S(2)}) %copy-start.4) | copy-done | bytes 32792
  6.1 0.0 copy-start.5
  6.2 0.7 copy-done.5
  6.8 0.0 copy-start.6
  6.8 0.7 copy-done.6
  7.5 62.9 %blend.1.ext = f32[40,48,128]{2,1,0:T(8,128)S(1)} custom-call(f32[32,32,128]{2,1,0:T(8,128)S(1)} %copy-done.1, bf16[4,64,2048]{2,1,0:T(8,128)(2,1)S(1)} %bitcast.11, s32[4,2048]{1,0:T(4,128)S(1)} %bitcast.13, s32[4]{0:T(128)S(1)} %bitcast.17, bf16[64,256]{1,0:T(8,128)(2,1)S(1)} %bitcast.14, bf16[4,256,256]{2,1,0:T(8,128)(2,1)S(1)} %bitcast.12, ...), custom_call_target="tpu_custom_call" | custom-call | tf_op jit(solution)/shard_map/blend/pallas_call | solution.py:273
  70.4 4.0 %finish.1 = (f32[32,32,128]{2,1,0:T(8,128)}, f32[3,32,32,128]{3,2,1,0:T(8,128)}) custom-call(f32[40,48,128]{2,1,0:T(8,128)S(1)} %blend.1.ext), custom_call_target="tpu_custom_call" | custom-call | tf_op jit(solution)/shard_map/finish/pallas_call | solution.py:299
Async XLA Ops:
  1.3 1.2 %copy-start = (bf16[1,1,4,2048,64]{3,4,2,1,0:T(8,128)(2,1)S(1)}, bf16[1,1,4,2048,64]{3,4,2,1,0:T(8,128)(2,1)}, u32[]{:S(2)}) copy-start(bf16[1,1,4,2048,64]{3,4,2,1,0:T(8,128)(2,1)} %param.9) | copy-start | bytes 3145732
  2.5 1.0 %copy-start.1 = (f32[32,32,128]{2,1,0:T(8,128)S(1)}, f32[32,32,128]{2,1,0:T(8,128)}, u32[]{:S(2)}) copy-start(f32[32,32,128]{2,1,0:T(8,128)} %dens.1) | copy-start | bytes 1572868
  3.6 1.0 %copy-start.2 = (bf16[1,1,4,256,256]{4,3,2,1,0:T(8,128)(2,1)S(1)}, bf16[1,1,4,256,256]{4,3,2,1,0:T(8,128)(2,1)}, u32[]{:S(2)}) copy-start(bf16[1,1,4,256,256]{4,3,2,1,0:T(8,128)(2,1)} %param.13) | copy-start | bytes 1572868
  4.6 0.8 %copy-start.3 = (s32[1,1,4,2048]{3,2,1,0:T(4,128)S(1)}, s32[1,1,4,2048]{3,2,1,0:T(4,128)}, u32[]{:S(2)}) copy-start(s32[1,1,4,2048]{3,2,1,0:T(4,128)} %param.10) | copy-start | bytes 98308
  5.4 0.8 %copy-start.4 = (bf16[1,1,64,256]{3,2,1,0:T(8,128)(2,1)S(1)}, bf16[1,1,64,256]{3,2,1,0:T(8,128)(2,1)}, u32[]{:S(2)}) copy-start(bf16[1,1,64,256]{3,2,1,0:T(8,128)(2,1)} %param.12) | copy-start | bytes 98308
  6.1 0.7 copy-start.5
  6.8 0.7 copy-start.6

commit v2 on v1

v2 whole, which is shorter than its diff:
```python
import functools

import jax
import jax.numpy as jnp
from jax import lax
from jax.experimental import pallas as pl
from jax.experimental.pallas import tpu as pltpu
from jax.sharding import PartitionSpec as P

MESH = pl.DeviceIdType.MESH
F32, BF16, I32 = jnp.float32, jnp.bfloat16, jnp.int32
HX, HY = 4, 8
GROUP = 4
ROUTES = (2, 1, 2, 1)
ROW_PARTS = 1
AROUND = ((-1, 0), (1, 0), (0, -1), (0, 1), (-1, -1), (-1, 1), (1, -1), (1, 1))


def spread(row, index):
    wide = jnp.broadcast_to(row, index.shape)
    return jnp.take_along_axis(wide, index, axis=1, mode="promise_in_bounds")


def blend_kernel(
    dens, feat, cell, count, w_in, w_hid, w_out, bias, out,
    field, coef_x, coef_y, recv, cells, tile_lo, tile_hi, tiles_in, cells_in, table,
    nets, up, down, left, right, values_in, values,
    cell_v, count_s, win_v, whid_v, wout_v, bias_v, win_t, whid_t, bias_w,
    relayed, load_sem, far_send, far_recv, relay_send, relay_recv, feat_send, feat_recv, dens_send, dens_recv, cell_send, cell_recv, value_send, value_recv,
):
    ix, iy = lax.axis_index("bx"), lax.axis_index("by")
    nx, ny = lax.axis_size("bx"), lax.axis_size("by")
    size_x, size_y, size_z = dens.shape
    listed = cell.shape[1]
    rows = listed // 128
    wide = size_x + 2 * HX
    base_2, base_3 = wide, wide + wide // 2

    def there(dx, dy):
        ok_x = jnp.bool_(True) if dx == 0 else (ix + dx >= 0 if dx < 0 else ix + dx < nx)
        ok_y = jnp.bool_(True) if dy == 0 else (iy + dy >= 0 if dy < 0 else iy + dy < ny)
        return ok_x & ok_y

    def at(dx, dy):
        return {"bx": ix + dx, "by": iy + dy}

    loads = [
        pltpu.make_async_copy(src, dst, load_sem.at[n])
        for n, (src, dst) in enumerate(
            ((cell, cell_v), (count, count_s), (w_hid, whid_v), (w_in, win_v), (w_out, wout_v), (bias, bias_v),
             (dens, field.at[pl.ds(HX, size_x), pl.ds(HY, size_y), :]))
        )
    ]
    field[0:HX] = jnp.zeros_like(field[0:HX])
    field[HX + size_x :] = jnp.zeros_like(field[HX + size_x :])
    field[HX : HX + size_x, 0:HY, :] = jnp.zeros((size_x, HY, size_z), F32)
    field[HX : HX + size_x, HY + size_y :, :] = jnp.zeros((size_x, HY, size_z), F32)
    values_in[...] = jnp.zeros_like(values_in)
    nets[...] = jnp.zeros_like(nets)
    tiles_in[...] = jnp.full_like(tiles_in, -1)
    cells_in[...] = jnp.full_like(cells_in, -1)
    for load in loads:
        load.start()
    place_in = ix % GROUP
    flows = []
    for step, first in ((1, GROUP - 1), (-1, 0)):
        def starts(shift, step=step, first=first):
            origin = ix + shift
            return (origin % GROUP == first) & (origin >= 0) & (origin < nx) & (origin + step >= 0) & (origin + step < nx)

        flows.append((step, 1 if step > 0 else 0, starts))
    behind = sorted({r for r in ROUTES if r})
    expected = sum(there(dx, dy).astype(I32) for dx, dy in AROUND)
    barrier = pltpu.get_barrier_semaphore()
    for dx, dy in AROUND:
        @pl.when(there(dx, dy))
        def _(dx=dx, dy=dy):
            pl.semaphore_signal(barrier, inc=1, device_id=at(dx, dy), device_id_type=MESH)

    for step, _side, starts in flows:
        for r in behind:
            if r > 1:
                @pl.when(starts(r * step))
                def _(r=r, step=step):
                    pl.semaphore_signal(barrier, inc=1, device_id=at(r * step, 0), device_id_type=MESH)

                expected = expected + starts(0).astype(I32)

            @pl.when(starts(-step))
            def _(r=r, step=step):
                pl.semaphore_signal(barrier, inc=1, device_id=at(-(r + 1) * step, 0), device_id_type=MESH)

            expected = expected + starts(r * step).astype(I32)

    loads[0].wait()
    loads[1].wait()
    ranks = lax.broadcasted_iota(I32, (1, listed), 1)
    for s in range(4):
        usable = (ranks < count_s[0, s]) & there(*AROUND[s])
        height = jnp.where(usable, cell_v[s : s + 1, :] & (size_z - 1), -1)
        for r in range(rows):
            cells[s * rows + r : s * rows + r + 1, :] = height[:, r * 128 : (r + 1) * 128]
    pairs = HX // 2
    tile_lo[0:HX] = cells[0:HX]
    tile_hi[0:HX] = cells[2 * rows - HX : 2 * rows]
    for n, s in enumerate((2, 3)):
        tile_lo[HX + n * pairs : HX + (n + 1) * pairs] = cells[s * rows : s * rows + pairs]
        tile_hi[HX + n * pairs : HX + (n + 1) * pairs] = cells[(s + 1) * rows - pairs : (s + 1) * rows]

    def fill(which, source):
        table[which, HX : HX + size_x] = source[0 : 2 * rows]
        for n, base in enumerate((base_2, base_3)):
            table[which, base + pairs : base + pairs + rows] = source[(2 + n) * rows : (3 + n) * rows]

    def fill_strips(which, lo, hi):
        table[which, 0:HX] = lo[0:HX]
        table[which, HX + size_x : wide] = hi[0:HX]
        for n, base in enumerate((base_2, base_3)):
            table[which, base : base + pairs] = lo[HX + n * pairs : HX + (n + 1) * pairs]
            table[which, base + pairs + rows : base + rows + 2 * pairs] = hi[HX + n * pairs : HX + (n + 1) * pairs]

    lane = lax.broadcasted_iota(I32, (8, 128), 1)
    sub = lax.broadcasted_iota(I32, (8, 128), 0)
    groups = size_y // 8
    half = groups // 2
    index = [4 * (8 * g + sub) + lane // 32 for g in range(groups)]
    dist_y = [((8 * g + sub).astype(F32) + 0.5) / size_y - 0.5 for g in range(groups)]
    own_groups = [(0, g, HY + 8 * g) for g in range(groups)]
    side_groups = [(1, groups - 1, 0), (2, 0, HY + size_y)]

    def entries(lists, which, g, pair, parity):
        row_x = lists[which, pl.ds(2 * pair + parity, 1), :]
        row_y = lists[which, pl.ds((base_2 if g < half else base_3) + pair, 1), :]
        return spread(row_x, index[g]), spread(row_y, index[g % half + half * parity])

    def prepare(chosen):
        def step(pair, _):
            for parity in range(2):
                x = 2 * pair + parity
                local = (x + size_x - HX) % size_x
                dist_x = (local.astype(F32) + 0.5) / size_x - 0.5
                off_x = jnp.where(local < size_x // 2, -1.0, 1.0)
                for which, g, place in chosen:
                    in_x, in_y = entries(table, which, g, pair, parity)
                    off_y = -1.0 if g < half else 1.0
                    sq_x, sq_y = dist_x * dist_x, dist_y[g] * dist_y[g]
                    far_x, far_y = dist_x - off_x, dist_y[g] - off_y
                    own = 1.0 / (sq_x + sq_y + 0.25)
                    w_x = jnp.where(in_x == lane, 1.0 / (far_x * far_x + sq_y + 0.25), 0.0)
                    w_y = jnp.where(in_y == lane, 1.0 / (sq_x + far_y * far_y + 0.25), 0.0)
                    share = 1.0 / (own + w_x + w_y)
                    voxels = pl.ds(place, 8)
                    field[x, voxels, :] = own * field[x, voxels, :] * share
                    coef_x[x, voxels, :] = w_x * share
                    coef_y[x, voxels, :] = w_y * share
            return 0

        return step

    fill(0, cells)
    for load in loads[2:]:
        load.wait()
    lax.fori_loop(pairs, wide // 2 - pairs, prepare(own_groups), 0)
    for layer in range(w_hid.shape[0]):
        whid_t[layer] = whid_v[layer].T
    win_t[...] = win_v[...].T
    for layer in range(bias.shape[0]):
        bias_w[layer] = jnp.broadcast_to(bias_v[layer], (128, bias.shape[2])).T

    pl.semaphore_wait(barrier, expected)

    def remote(src, dst, send, arrive, n, dx, dy):
        return pltpu.make_async_remote_copy(
            src_ref=src, dst_ref=dst, send_sem=send.at[n], recv_sem=arrive.at[n],
            device_id=at(dx, dy), device_id_type=MESH)

    def opposite(s):
        dx = jnp.where(s == 0, 1, jnp.where(s == 1, -1, 0))
        dy = jnp.where(s == 2, 1, jnp.where(s == 3, -1, 0))
        ok = (ix + dx >= 0) & (ix + dx < nx) & (iy + dy >= 0) & (iy + dy < ny)
        return ok, dx, dy

    def feature_copy(s, dx, dy):
        return remote(feat.at[s], recv.at[s], feat_send, feat_recv, s, dx, dy)

    def cut(d, own, width, inner):
        if d == 0:
            return pl.ds(0, inner), pl.ds(own, inner)
        if d > 0:
            return pl.ds(inner - width, width), pl.ds(own - width, width)
        return pl.ds(0, width), pl.ds(own + inner, width)

    def density_copy(n, dx, dy):
        src_x, dst_x = cut(dx, HX, HX, size_x)
        src_y, dst_y = cut(dy, HY, HY, size_y)
        return remote(
            dens.at[src_x, src_y, :], field.at[dst_x, dst_y, :], dens_send, dens_recv, n, dx, dy
        )

    def cell_copy(n, dx, dy):
        m = AROUND.index((-dx, -dy))
        if dx == 0:
            return remote(cells, cells_in.at[m - 2], cell_send, cell_recv, n, dx, dy)
        return remote(tile_lo if dx < 0 else tile_hi, tiles_in.at[m], cell_send, cell_recv, n, dx, dy)

    def value_copy(n, dx, dy):
        m = AROUND.index((-dx, -dy))
        src = (left if dy < 0 else right) if dx == 0 else (down if dx < 0 else up)
        return remote(src, values_in.at[m], value_send, value_recv, n, dx, dy)

    part_rows = feat.shape[1] // ROW_PARTS
    part_columns = listed * ROW_PARTS // len(ROUTES)

    def piece(ref, s, n):
        return ref.at[
            s, pl.ds(n % ROW_PARTS * part_rows, part_rows), pl.ds(n // ROW_PARTS * part_columns, part_columns)
        ]

    def far_copy(n, side, step):
        r = ROUTES[n]
        if r:
            dst, arrive, shift = relayed.at[side, n], relay_recv.at[side, n], -r * step
        else:
            dst, arrive, shift = piece(recv, side, n), far_recv.at[n], step
        return pltpu.make_async_remote_copy(
            src_ref=piece(feat, side, n), dst_ref=dst, send_sem=far_send.at[n], recv_sem=arrive,
            device_id=at(shift, 0), device_id_type=MESH)

    def forward_copy(n, side, step):
        return pltpu.make_async_remote_copy(
            src_ref=relayed.at[side, n], dst_ref=piece(recv, side, n), send_sem=relay_send.at[side, n],
            recv_sem=far_recv.at[n], device_id=at((ROUTES[n] + 1) * step, 0), device_id_type=MESH)

    for step, side, starts in flows:
        @pl.when(starts(0))
        def _(step=step, side=side):
            for n in range(len(ROUTES)):
                far_copy(n, side, step).start()

    def near(s):
        ok = there(*AROUND[s])
        for step, side, starts in flows:
            if s == side:
                ok = ok & jnp.logical_not(starts(0))
        return ok

    for s in (2, 3, 0, 1):
        @pl.when(near(s))
        def _(s=s):
            feature_copy(s, *AROUND[s]).start()

    for n in range(len(ROUTES)):
        for step, side, starts in flows:
            if ROUTES[n]:
                @pl.when(starts(ROUTES[n] * step))
                def _(n=n, step=step, side=side):
                    far_copy(n, side, step).wait_recv()
                    forward_copy(n, side, step).start()

    for n, (dx, dy) in enumerate(AROUND):
        @pl.when(there(dx, dy))
        def _(n=n, dx=dx, dy=dy):
            cell_copy(n, dx, dy).start()
            density_copy(n, dx, dy).start()

    head = jnp.broadcast_to(wout_v[...].astype(F32), (16, w_out.shape[1])).astype(BF16)
    last = ix % 4 == 3

    def evaluate(step, _):
        s = jnp.where(step < 2, step + 2, jnp.where(last, 3 - step, step - 2))
        ok, dx, dy = opposite(s)

        @pl.when(ok)
        def _():
            far = ((s == 1) & flows[0][2](-1)) | ((s == 0) & flows[1][2](1))

            @pl.when(far)
            def _():
                for n in range(len(ROUTES)):
                    pltpu.make_async_remote_copy(
                        src_ref=piece(recv, s, n), dst_ref=piece(recv, s, n), send_sem=far_send.at[n],
                        recv_sem=far_recv.at[n], device_id=at(dx, dy), device_id_type=MESH).wait_recv()

            @pl.when(jnp.logical_not(far))
            def _():
                feature_copy(s, dx, dy).wait_recv()

            def layer(weights, hidden, level):
                column = jnp.concatenate([bias_w[level]] * (listed // 128), axis=1)
                total = jnp.dot(weights, hidden, preferred_element_type=F32) + column
                return jnp.maximum(total.astype(BF16), 0)

            hidden = layer(win_t[...], recv[s], 0)
            for level in range(whid_t.shape[0]):
                hidden = layer(whid_t[level], hidden, level + 1)
            raw = jnp.dot(head, hidden, preferred_element_type=F32)[0:1, :]
            result = jnp.maximum(raw, 0.0) + jnp.log1p(jnp.exp(-jnp.abs(raw)))
            for r in range(rows):
                nets[s, r : r + 1, :] = result[:, r * 128 : (r + 1) * 128]

        return 0

    lax.fori_loop(0, 4, evaluate, 0)

    up[0:rows] = nets[0]
    down[0:rows] = nets[1]
    left[0:rows] = nets[3]
    right[0:rows] = nets[2]
    for n, s in enumerate((2, 3)):
        up[rows + n * pairs : rows + (n + 1) * pairs] = nets[s, rows - pairs : rows]
        down[rows + n * pairs : rows + (n + 1) * pairs] = nets[s, 0:pairs]
    for side in (left, right):
        side[rows : rows + HX] = nets[0, 0:HX]
        side[rows + HX : rows + 2 * HX] = nets[1, rows - HX : rows]
    for n, (dx, dy) in enumerate(AROUND):
        @pl.when(there(dx, dy))
        def _(n=n, dx=dx, dy=dy):
            value_copy(n, dx, dy).start()

    for n, (dx, dy) in enumerate(AROUND):
        @pl.when(there(-dx, -dy))
        def _(n=n, dx=dx, dy=dy):
            cell_copy(n, dx, dy).wait_recv()
            density_copy(n, dx, dy).wait_recv()

    fill(1, cells_in.at[0])
    fill(2, cells_in.at[1])
    fill_strips(0, tiles_in.at[0], tiles_in.at[1])
    fill_strips(1, tiles_in.at[4], tiles_in.at[6])
    fill_strips(2, tiles_in.at[5], tiles_in.at[7])
    lax.fori_loop(0, pairs, prepare(own_groups), 0)
    lax.fori_loop(wide // 2 - pairs, wide // 2, prepare(own_groups), 0)
    lax.fori_loop(0, wide // 2, prepare(side_groups), 0)

    for n, (dx, dy) in enumerate(AROUND):
        @pl.when(there(-dx, -dy))
        def _(n=n, dx=dx, dy=dy):
            value_copy(n, dx, dy).wait_recv()

    def put(which, first, source):
        values[which, first : first + source.shape[0]] = source

    tail, strip = HX + size_x, rows
    lo_2, hi_2 = base_2 + pairs, base_2 + pairs + rows
    lo_3, hi_3 = base_3 + pairs, base_3 + pairs + rows
    west, east, south, north = (values_in.at[m] for m in range(4))
    south_west, north_west, south_east, north_east = (values_in.at[m] for m in range(4, 8))
    put(0, HX, west[0:rows])
    put(0, HX + rows, east[0:rows])
    put(0, 0, nets[1, rows - HX : rows])
    put(0, tail, nets[0, 0:HX])
    put(0, lo_2, south[0:rows])
    put(0, lo_3, north[0:rows])
    put(0, base_2, south_west[strip : strip + pairs])
    put(0, base_3, north_west[strip + pairs : strip + 2 * pairs])
    put(0, hi_2, south_east[strip : strip + pairs])
    put(0, hi_3, north_east[strip + pairs : strip + 2 * pairs])
    for which, column, to_west, to_east in ((1, south, south_west, south_east), (2, north, north_west, north_east)):
        put(which, HX, to_west[0:rows])
        put(which, HX + rows, to_east[0:rows])
        put(which, 0, column[strip + HX : strip + 2 * HX])
        put(which, tail, column[strip : strip + HX])
    put(1, lo_3, nets[3])
    put(1, base_3, west[strip + pairs : strip + 2 * pairs])
    put(1, hi_3, east[strip + pairs : strip + 2 * pairs])
    put(2, lo_2, nets[2])
    put(2, base_2, west[strip : strip + pairs])
    put(2, hi_2, east[strip : strip + pairs])

    def blend(pair, _):
        for parity in range(2):
            x = 2 * pair + parity
            for which, g, place in own_groups + side_groups:
                from_x, from_y = entries(values, which, g, pair, parity)
                voxels = pl.ds(place, 8)
                out[x, voxels, :] = (
                    field[x, voxels, :] + coef_x[x, voxels, :] * from_x + coef_y[x, voxels, :] * from_y
                )
        return 0

    lax.fori_loop(0, wide // 2, blend, 0)

    for s in range(4):
        @pl.when(near(s))
        def _(s=s):
            feature_copy(s, *AROUND[s]).wait_send()

    for step, side, starts in flows:
        @pl.when(starts(0))
        def _(step=step, side=side):
            for n in range(len(ROUTES)):
                far_copy(n, side, step).wait_send()

        for n in range(len(ROUTES)):
            if ROUTES[n]:
                @pl.when(starts(ROUTES[n] * step))
                def _(n=n, step=step, side=side):
                    forward_copy(n, side, step).wait_send()

    for n, (dx, dy) in enumerate(AROUND):
        @pl.when(there(dx, dy))
        def _(n=n, dx=dx, dy=dy):
            cell_copy(n, dx, dy).wait_send()
            density_copy(n, dx, dy).wait_send()
            value_copy(n, dx, dy).wait_send()


def finish_kernel(ext, smoothed, normals, one, two):
    ix, iy = lax.axis_index("bx"), lax.axis_index("by")
    nx, ny = lax.axis_size("bx"), lax.axis_size("by")
    size_x, size_y, size_z = smoothed.shape
    full_x, full_y = size_x + 2 * HX, size_y + 2 * HY
    sub = lax.broadcasted_iota(I32, (full_y, size_z), 0)
    inside_y = ((sub >= HY) | (iy > 0)) & ((sub < HY + size_y) | (iy < ny - 1))
    keep_y = jnp.where(inside_y, 0.2, 0.0)

    def one_pass(src, dst, margin):
        def step(x, _):
            centre = src[x]
            total = (
                centre + src[x + 1] + src[x - 1]
                + pltpu.roll(centre, 1, 0) + pltpu.roll(centre, full_y - 1, 0)
            )
            inside = ((x >= HX) | (ix > 0)) & ((x < HX + size_x) | (ix < nx - 1))
            dst[x] = total * jnp.where(inside, keep_y, 0.0)
            return 0

        lax.fori_loop(margin, full_x - margin, step, 0, unroll=2)

    one_pass(ext, one, 1)
    one_pass(one, two, 2)
    one_pass(two, one, 3)
    last_z = lax.broadcasted_iota(I32, (size_y, size_z), 1)

    def gradient(x, _):
        row = HX + x
        centre = one[row]
        own = centre[HY : HY + size_y]
        grad_x = one[row + 1, HY : HY + size_y, :] - one[row - 1, HY : HY + size_y, :]
        grad_y = (pltpu.roll(centre, full_y - 1, 0) - pltpu.roll(centre, 1, 0))[HY : HY + size_y]
        after = jnp.where(last_z == size_z - 1, 0.0, pltpu.roll(own, size_z - 1, 1))
        before = jnp.where(last_z == 0, 0.0, pltpu.roll(own, 1, 1))
        grad_z = after - before
        factor = lax.rsqrt(1.0 + grad_x * grad_x + grad_y * grad_y + grad_z * grad_z)
        smoothed[x] = own
        normals[0, x] = grad_x * factor
        normals[1, x] = grad_y * factor
        normals[2, x] = grad_z * factor
        return 0

    lax.fori_loop(0, size_x, gradient, 0, unroll=2)


def shards(density, band_feat, band_cell, band_count, w_in, w_hid, w_out, biases):
    size_x, size_y, size_z = density.shape
    feat = jnp.swapaxes(band_feat[0, 0], 1, 2)
    sides, width, listed = feat.shape
    levels, hidden = w_hid.shape[2], w_hid.shape[3]
    rows = listed // 128
    full = (size_x + 2 * HX, size_y + 2 * HY, size_z)
    vmem = pl.BlockSpec(memory_space=pltpu.VMEM)
    hbm = pl.BlockSpec(memory_space=pltpu.HBM)
    dma = pltpu.SemaphoreType.DMA
    own_cells = (sides * rows, 128)
    message = (rows + 2 * HX, 128)
    tables = (3, 2 * full[0], 128)
    ext = pl.pallas_call(
        blend_kernel,
        out_shape=jax.ShapeDtypeStruct(full, F32),
        in_specs=[hbm] * 8,
        out_specs=vmem,
        scratch_shapes=[
            pltpu.VMEM(full, F32),
            pltpu.VMEM(full, F32),
            pltpu.VMEM(full, F32),
            pltpu.VMEM((sides, width, listed), BF16),
            pltpu.VMEM(own_cells, I32),
            pltpu.VMEM((2 * HX, 128), I32),
            pltpu.VMEM((2 * HX, 128), I32),
            pltpu.VMEM((8, 2 * HX, 128), I32),
            pltpu.VMEM((2,) + own_cells, I32),
            pltpu.VMEM(tables, I32),
            pltpu.VMEM((sides, rows, 128), F32),
            pltpu.VMEM(message, F32),
            pltpu.VMEM(message, F32),
            pltpu.VMEM(message, F32),
            pltpu.VMEM(message, F32),
            pltpu.VMEM((8,) + message, F32),
            pltpu.VMEM(tables, F32),
            pltpu.VMEM((sides, listed), I32),
            pltpu.SMEM((1, sides), I32),
            pltpu.VMEM((width, hidden), BF16),
            pltpu.VMEM((levels, hidden, hidden), BF16),
            pltpu.VMEM((1, hidden), BF16),
            pltpu.VMEM((levels + 1, 1, hidden), F32),
            pltpu.VMEM((hidden, width), BF16),
            pltpu.VMEM((levels, hidden, hidden), BF16),
            pltpu.VMEM((levels + 1, hidden, 128), F32),
            pltpu.VMEM((2, len(ROUTES), width // ROW_PARTS, listed * ROW_PARTS // len(ROUTES)), BF16),
            dma((7,)), dma((len(ROUTES),)), dma((len(ROUTES),)), dma((2, len(ROUTES))), dma((2, len(ROUTES))),
            dma((sides,)), dma((sides,)),
            dma((8,)), dma((8,)), dma((8,)), dma((8,)), dma((8,)), dma((8,)),
        ],
        compiler_params=pltpu.CompilerParams(
            collective_id=0, has_side_effects=True, vmem_limit_bytes=61 << 20
        ),
        name="blend",
    )(
        density, feat, band_cell[0, 0], band_count[0], w_in[0, 0], w_hid[0, 0],
        w_out[0], biases[0, 0][:, None, :],
    )
    return pl.pallas_call(
        finish_kernel,
        out_shape=(
            jax.ShapeDtypeStruct(density.shape, F32),
            jax.ShapeDtypeStruct((3,) + density.shape, F32),
        ),
        in_specs=[vmem],
        out_specs=(vmem, vmem),
        scratch_shapes=[pltpu.VMEM(full, F32), pltpu.VMEM(full, F32)],
        compiler_params=pltpu.CompilerParams(vmem_limit_bytes=32 << 20),
        name="finish",
    )(ext)


def solution(mesh):
    placed = (
        P("bx", "by", None),
        P("bx", "by", None, None, None),
        P("bx", "by", None, None),
        P("bx", "by", None),
        P("bx", "by", None, None),
        P("bx", "by", None, None, None),
        P("bx", "by", None),
        P("bx", "by", None, None),
    )
    return jax.shard_map(
        shards,
        mesh=mesh,
        in_specs=placed,
        out_specs=(P("bx", "by", None), P(None, "bx", "by", None)),
        check_vma=False,
    )
```

time: 74.8 us -> 50.4 us (0.67)
  the two profiles are of different devices: /device:TPU:159 before, /device:TPU:153 now
where the time goes in v2:
time: 50.4 us; the launch traced here: 50.3 us
  Pallas kernels  48.4 us (96%)
  local copies, waits for them, and re-layouts  1.19 us (2%)
  between operations  0.65 us (1%)
    pallas_call x1, Pallas kernels, shards(): pl.pallas_call(blend_kernel, out_shape=jax.ShapeDtypeStruct(full, F32), i...  44.4 us
    pallas_call x1, Pallas kernels, shards(): pl.pallas_call(finish_kernel, out_shape=(jax.ShapeDtypeStruct(density.sha...  3.97 us
    unnamed x2, local copies, waits for them, and re-layouts  1.19 us

profile of v2, /device:TPU:153, one launch (start us, length us, event | category | flops | bytes accessed | tf_op | source)
XLA Modules:
  0.0 50.3 jit_solution(6220585730543350256)
XLA Ops:
  0.6 44.4 %blend.1.ext = f32[40,48,128]{2,1,0:T(8,128)} custom-call(f32[32,32,128]{2,1,0:T(8,128)} %dens.1, bf16[4,64,2048]{2,1,0:T(8,128)(2,1)} %bitcast.9, s32[4,2048]{1,0:T(4,128)} %bitcast.11, s32[1,4]{1,0:T(1,128)} %bitcast.15, bf16[64,256]{1,0:T(8,128)(2,1)} %bitcast.12, bf16[4,256,256]{2,1,0:T(8,128)(2,1)} %bitcast.10, bf16[1,256]{1,0:T(2,128)(2,1)} %bitcast.14, ...), custom_call_target="tpu_custom_call" | custom-call | tf_op jit(solution)/shard_map/blend/pallas_call | solution.py:467
  45.1 0.0 copy-start
  45.1 1.2 %copy-done = f32[40,48,128]{2,1,0:T(8,128)S(1)} copy-done((f32[40,48,128]{2,1,0:T(8,128)S(1)}, f32[40,48,128]{2,1,0:T(8,128)}, u32[]{:S(2)}) %copy-start) | copy-done | bytes 983064
  46.3 4.0 %finish.1 = (f32[32,32,128]{2,1,0:T(8,128)}, f32[3,32,32,128]{3,2,1,0:T(8,128)}) custom-call(f32[40,48,128]{2,1,0:T(8,128)S(1)} %copy-done), custom_call_target="tpu_custom_call" | custom-call | tf_op jit(solution)/shard_map/finish/pallas_call | solution.py:512
Async XLA Ops:
  45.1 1.2 %copy-start = (f32[40,48,128]{2,1,0:T(8,128)S(1)}, f32[40,48,128]{2,1,0:T(8,128)}, u32[]{:S(2)}) copy-start(f32[40,48,128]{2,1,0:T(8,128)} %blend.1.ext) | copy-start | bytes 2949124

commit v3 on v2

--- a/solution.py
+++ b/solution.py
@@ -11,8 +11,8 @@
 F32, BF16, I32 = jnp.float32, jnp.bfloat16, jnp.int32
 HX, HY = 4, 8
 GROUP = 4
-ROUTES = (2, 1, 2, 1)
-ROW_PARTS = 1
+ROUTES = (2, 1, 2, 1, 0, 2, 1, 2)
+ROW_PARTS = 2
 AROUND = ((-1, 0), (1, 0), (0, -1), (0, 1), (-1, -1), (-1, 1), (1, -1), (1, 1))
 
 
@@ -23,10 +23,10 @@
 
 def blend_kernel(
     dens, feat, cell, count, w_in, w_hid, w_out, bias, out,
-    field, coef_x, coef_y, recv, cells, tile_lo, tile_hi, tiles_in, cells_in, table,
+    field, side_after, side_before, coef_x, coef_y, recv, cells, tile_lo, tile_hi, tiles_in, cells_in, table,
     nets, up, down, left, right, values_in, values,
     cell_v, count_s, win_v, whid_v, wout_v, bias_v, win_t, whid_t, bias_w,
-    relayed, load_sem, far_send, far_recv, relay_send, relay_recv, feat_send, feat_recv, dens_send, dens_recv, cell_send, cell_recv, value_send, value_recv,
+    relayed, load_sem, far_send, far_recv, relay_send, relay_recv, feat_send, feat_recv, dens_send, dens_recv, cell_send, cell_recv, value_send, value_recv, out_sem,
 ):
     ix, iy = lax.axis_index("bx"), lax.axis_index("by")
     nx, ny = lax.axis_size("bx"), lax.axis_size("by")
@@ -48,13 +48,13 @@
         pltpu.make_async_copy(src, dst, load_sem.at[n])
         for n, (src, dst) in enumerate(
             ((cell, cell_v), (count, count_s), (w_hid, whid_v), (w_in, win_v), (w_out, wout_v), (bias, bias_v),
-             (dens, field.at[pl.ds(HX, size_x), pl.ds(HY, size_y), :]))
+             (dens, field.at[pl.ds(HX, size_x), pl.ds(0, size_y), :]))
         )
     ]
     field[0:HX] = jnp.zeros_like(field[0:HX])
     field[HX + size_x :] = jnp.zeros_like(field[HX + size_x :])
-    field[HX : HX + size_x, 0:HY, :] = jnp.zeros((size_x, HY, size_z), F32)
-    field[HX : HX + size_x, HY + size_y :, :] = jnp.zeros((size_x, HY, size_z), F32)
+    side_after[...] = jnp.zeros_like(side_after)
+    side_before[...] = jnp.zeros_like(side_before)
     values_in[...] = jnp.zeros_like(values_in)
     nets[...] = jnp.zeros_like(nets)
     tiles_in[...] = jnp.full_like(tiles_in, -1)
@@ -125,13 +125,27 @@
     half = groups // 2
     index = [4 * (8 * g + sub) + lane // 32 for g in range(groups)]
     dist_y = [((8 * g + sub).astype(F32) + 0.5) / size_y - 0.5 for g in range(groups)]
-    own_groups = [(0, g, HY + 8 * g) for g in range(groups)]
-    side_groups = [(1, groups - 1, 0), (2, 0, HY + size_y)]
-
-    def entries(lists, which, g, pair, parity):
-        row_x = lists[which, pl.ds(2 * pair + parity, 1), :]
-        row_y = lists[which, pl.ds((base_2 if g < half else base_3) + pair, 1), :]
-        return spread(row_x, index[g]), spread(row_y, index[g % half + half * parity])
+    after = sub < HX
+
+    def both(first, second):
+        return jnp.where(after, first, second)
+
+    top = groups - 1
+    index_side = both(index[0], index[top])
+    index_side_y = [both(index[half * parity], index[top % half + half * parity]) for parity in range(2)]
+    dist_side, off_side = both(dist_y[0], dist_y[top]), both(-1.0, 1.0)
+
+    def entries(lists, g, pair, parity):
+        def row(which, at_row):
+            return lists[which, pl.ds(at_row, 1), :]
+
+        x = 2 * pair + parity
+        if g < groups:
+            row_y = row(0, (base_2 if g < half else base_3) + pair)
+            return spread(row(0, x), index[g]), spread(row_y, index[g % half + half * parity])
+        row_x = both(row(2, x), row(1, x))
+        row_y = both(row(2, base_2 + pair), row(1, base_3 + pair))
+        return spread(row_x, index_side), spread(row_y, index_side_y[parity])
 
     def prepare(chosen):
         def step(pair, _):
@@ -140,23 +154,29 @@
                 local = (x + size_x - HX) % size_x
                 dist_x = (local.astype(F32) + 0.5) / size_x - 0.5
                 off_x = jnp.where(local < size_x // 2, -1.0, 1.0)
-                for which, g, place in chosen:
-                    in_x, in_y = entries(table, which, g, pair, parity)
-                    off_y = -1.0 if g < half else 1.0
-                    sq_x, sq_y = dist_x * dist_x, dist_y[g] * dist_y[g]
-                    far_x, far_y = dist_x - off_x, dist_y[g] - off_y
+                for g in chosen:
+                    in_x, in_y = entries(table, g, pair, parity)
+                    voxels = pl.ds(8 * g, 8)
+                    if g < groups:
+                        across, off_y = dist_y[g], -1.0 if g < half else 1.0
+                        density = field[x, voxels, :]
+                    else:
+                        across, off_y = dist_side, off_side
+                        density = both(side_after[x], side_before[x])
+                    sq_x, sq_y = dist_x * dist_x, across * across
+                    far_x, far_y = dist_x - off_x, across - off_y
                     own = 1.0 / (sq_x + sq_y + 0.25)
                     w_x = jnp.where(in_x == lane, 1.0 / (far_x * far_x + sq_y + 0.25), 0.0)
                     w_y = jnp.where(in_y == lane, 1.0 / (sq_x + far_y * far_y + 0.25), 0.0)
                     share = 1.0 / (own + w_x + w_y)
-                    voxels = pl.ds(place, 8)
-                    field[x, voxels, :] = own * field[x, voxels, :] * share
+                    field[x, voxels, :] = own * density * share
                     coef_x[x, voxels, :] = w_x * share
                     coef_y[x, voxels, :] = w_y * share
             return 0
 
         return step
 
+    own_groups = tuple(range(groups))
     fill(0, cells)
     for load in loads[2:]:
         load.wait()
@@ -183,19 +203,20 @@
     def feature_copy(s, dx, dy):
         return remote(feat.at[s], recv.at[s], feat_send, feat_recv, s, dx, dy)
 
-    def cut(d, own, width, inner):
-        if d == 0:
-            return pl.ds(0, inner), pl.ds(own, inner)
-        if d > 0:
-            return pl.ds(inner - width, width), pl.ds(own - width, width)
-        return pl.ds(0, width), pl.ds(own + inner, width)
-
     def density_copy(n, dx, dy):
-        src_x, dst_x = cut(dx, HX, HX, size_x)
-        src_y, dst_y = cut(dy, HY, HY, size_y)
-        return remote(
-            dens.at[src_x, src_y, :], field.at[dst_x, dst_y, :], dens_send, dens_recv, n, dx, dy
-        )
+        if dx == 0:
+            src_x, dst_x = pl.ds(0, size_x), pl.ds(HX, size_x)
+        elif dx > 0:
+            src_x, dst_x = pl.ds(size_x - HX, HX), pl.ds(0, HX)
+        else:
+            src_x, dst_x = pl.ds(0, HX), pl.ds(HX + size_x, HX)
+        if dy == 0:
+            src, dst = dens.at[src_x], field.at[dst_x, pl.ds(0, size_y), :]
+        elif dy > 0:
+            src, dst = dens.at[src_x, pl.ds(size_y - HY, HY), :], side_before.at[dst_x]
+        else:
+            src, dst = dens.at[src_x, pl.ds(0, HY), :], side_after.at[dst_x]
+        return remote(src, dst, dens_send, dens_recv, n, dx, dy)
 
     def cell_copy(n, dx, dy):
         m = AROUND.index((-dx, -dy))
@@ -249,8 +270,8 @@
         def _(s=s):
             feature_copy(s, *AROUND[s]).start()
 
-    for n in range(len(ROUTES)):
-        for step, side, starts in flows:
+    for step, side, starts in reversed(flows):
+        for n in range(len(ROUTES)):
             if ROUTES[n]:
                 @pl.when(starts(ROUTES[n] * step))
                 def _(n=n, step=step, side=side):
@@ -328,9 +349,9 @@
     fill_strips(0, tiles_in.at[0], tiles_in.at[1])
     fill_strips(1, tiles_in.at[4], tiles_in.at[6])
     fill_strips(2, tiles_in.at[5], tiles_in.at[7])
-    lax.fori_loop(0, pairs, prepare(own_groups), 0)
-    lax.fori_loop(wide // 2 - pairs, wide // 2, prepare(own_groups), 0)
-    lax.fori_loop(0, wide // 2, prepare(side_groups), 0)
+    lax.fori_loop(0, pairs, prepare(own_groups), 0, unroll=True)
+    lax.fori_loop(wide // 2 - pairs, wide // 2, prepare(own_groups), 0, unroll=True)
+    lax.fori_loop(0, wide // 2, prepare((groups,)), 0, unroll=5)
 
     for n, (dx, dy) in enumerate(AROUND):
         @pl.when(there(-dx, -dy))
@@ -367,18 +388,24 @@
     put(2, base_2, west[strip : strip + pairs])
     put(2, hi_2, east[strip : strip + pairs])
 
-    def blend(pair, _):
-        for parity in range(2):
-            x = 2 * pair + parity
-            for which, g, place in own_groups + side_groups:
-                from_x, from_y = entries(values, which, g, pair, parity)
-                voxels = pl.ds(place, 8)
-                out[x, voxels, :] = (
+    def result_copy(chunk):
+        part = pl.ds(8 * chunk, 8)
+        return pltpu.make_async_copy(field.at[part], out.at[part], out_sem.at[chunk])
+
+    def blend(chunk, _):
+        for k in range(8):
+            pair, parity = 4 * chunk + k // 2, k % 2
+            x = 8 * chunk + k
+            for g in range(groups + 1):
+                from_x, from_y = entries(values, g, pair, parity)
+                voxels = pl.ds(8 * g, 8)
+                field[x, voxels, :] = (
                     field[x, voxels, :] + coef_x[x, voxels, :] * from_x + coef_y[x, voxels, :] * from_y
                 )
+        result_copy(chunk).start()
         return 0
 
-    lax.fori_loop(0, wide // 2, blend, 0)
+    lax.fori_loop(0, wide // 8, blend, 0)
 
     for s in range(4):
         @pl.when(near(s))
@@ -403,18 +430,35 @@
             cell_copy(n, dx, dy).wait_send()
             density_copy(n, dx, dy).wait_send()
             value_copy(n, dx, dy).wait_send()
-
-
-def finish_kernel(ext, smoothed, normals, one, two):
+    for chunk in range(wide // 8):
+        result_copy(chunk).wait()
+
+
+def finish_kernel(ext, smoothed, normals, zero, one, two, soft, grads, load_sem, soft_sem, grad_sem):
     ix, iy = lax.axis_index("bx"), lax.axis_index("by")
     nx, ny = lax.axis_size("bx"), lax.axis_size("by")
     size_x, size_y, size_z = smoothed.shape
-    full_x, full_y = size_x + 2 * HX, size_y + 2 * HY
+    full_x, full_y = size_x + 2 * HX, size_y + HY
+    chunks = full_x // 8
+
+    def load(chunk):
+        part = pl.ds(8 * chunk, 8)
+        return pltpu.make_async_copy(ext.at[part], zero.at[part], load_sem.at[chunk])
+
+    def store(chunk):
+        part = pl.ds(8 * chunk, 8)
+        return (
+            pltpu.make_async_copy(soft.at[part], smoothed.at[part], soft_sem.at[chunk]),
+            pltpu.make_async_copy(grads.at[:, part], normals.at[:, part], grad_sem.at[chunk]),
+        )
+
+    for chunk in range(chunks):
+        load(chunk).start()
     sub = lax.broadcasted_iota(I32, (full_y, size_z), 0)
-    inside_y = ((sub >= HY) | (iy > 0)) & ((sub < HY + size_y) | (iy < ny - 1))
+    inside_y = (sub < size_y) | ((sub < size_y + HX) & (iy < ny - 1)) | ((sub >= size_y + HX) & (iy > 0))
     keep_y = jnp.where(inside_y, 0.2, 0.0)
 
-    def one_pass(src, dst, margin):
+    def one_pass(src, dst, first, end):
         def step(x, _):
             centre = src[x]
             total = (
@@ -425,30 +469,39 @@
             dst[x] = total * jnp.where(inside, keep_y, 0.0)
             return 0
 
-        lax.fori_loop(margin, full_x - margin, step, 0, unroll=2)
-
-    one_pass(ext, one, 1)
-    one_pass(one, two, 2)
-    one_pass(two, one, 3)
+        lax.fori_loop(first, end, step, 0, unroll=4)
+
+    for chunk in range(chunks):
+        load(chunk).wait()
+        one_pass(zero, one, max(1, 8 * chunk - 1), 8 * chunk + 7)
+    one_pass(one, two, 2, full_x - 2)
+    one_pass(two, one, 3, full_x - 3)
     last_z = lax.broadcasted_iota(I32, (size_y, size_z), 1)
 
-    def gradient(x, _):
-        row = HX + x
-        centre = one[row]
-        own = centre[HY : HY + size_y]
-        grad_x = one[row + 1, HY : HY + size_y, :] - one[row - 1, HY : HY + size_y, :]
-        grad_y = (pltpu.roll(centre, full_y - 1, 0) - pltpu.roll(centre, 1, 0))[HY : HY + size_y]
-        after = jnp.where(last_z == size_z - 1, 0.0, pltpu.roll(own, size_z - 1, 1))
-        before = jnp.where(last_z == 0, 0.0, pltpu.roll(own, 1, 1))
-        grad_z = after - before
-        factor = lax.rsqrt(1.0 + grad_x * grad_x + grad_y * grad_y + grad_z * grad_z)
-        smoothed[x] = own
-        normals[0, x] = grad_x * factor
-        normals[1, x] = grad_y * factor
-        normals[2, x] = grad_z * factor
+    def gradient(chunk, _):
+        for k in range(8):
+            x = 8 * chunk + k
+            row = HX + x
+            centre = one[row]
+            own = centre[0:size_y]
+            grad_x = one[row + 1, 0:size_y, :] - one[row - 1, 0:size_y, :]
+            grad_y = (pltpu.roll(centre, full_y - 1, 0) - pltpu.roll(centre, 1, 0))[0:size_y]
+            ahead = jnp.where(last_z == size_z - 1, 0.0, pltpu.roll(own, size_z - 1, 1))
+            behind = jnp.where(last_z == 0, 0.0, pltpu.roll(own, 1, 1))
+            grad_z = ahead - behind
+            factor = lax.rsqrt(1.0 + grad_x * grad_x + grad_y * grad_y + grad_z * grad_z)
+            soft[x] = own
+            grads[0, x] = grad_x * factor
+            grads[1, x] = grad_y * factor
+            grads[2, x] = grad_z * factor
+        for copy in store(chunk):
+            copy.start()
         return 0
 
-    lax.fori_loop(0, size_x, gradient, 0, unroll=2)
+    lax.fori_loop(0, size_x // 8, gradient, 0)
+    for chunk in range(size_x // 8):
+        for copy in store(chunk):
+            copy.wait()
 
 
 def shards(density, band_feat, band_cell, band_count, w_in, w_hid, w_out, biases):
@@ -457,8 +510,8 @@
     sides, width, listed = feat.shape
     levels, hidden = w_hid.shape[2], w_hid.shape[3]
     rows = listed // 128
-    full = (size_x + 2 * HX, size_y + 2 * HY, size_z)
-    vmem = pl.BlockSpec(memory_space=pltpu.VMEM)
+    full = (size_x + 2 * HX, size_y + HY, size_z)
+    beside = (size_x + 2 * HX, HY, size_z)
     hbm = pl.BlockSpec(memory_space=pltpu.HBM)
     dma = pltpu.SemaphoreType.DMA
     own_cells = (sides * rows, 128)
@@ -468,9 +521,11 @@
         blend_kernel,
         out_shape=jax.ShapeDtypeStruct(full, F32),
         in_specs=[hbm] * 8,
-        out_specs=vmem,
+        out_specs=hbm,
         scratch_shapes=[
             pltpu.VMEM(full, F32),
+            pltpu.VMEM(beside, F32),
+            pltpu.VMEM(beside, F32),
             pltpu.VMEM(full, F32),
             pltpu.VMEM(full, F32),
             pltpu.VMEM((sides, width, listed), BF16),
@@ -499,7 +554,7 @@
             pltpu.VMEM((2, len(ROUTES), width // ROW_PARTS, listed * ROW_PARTS // len(ROUTES)), BF16),
             dma((7,)), dma((len(ROUTES),)), dma((len(ROUTES),)), dma((2, len(ROUTES))), dma((2, len(ROUTES))),
             dma((sides,)), dma((sides,)),
-            dma((8,)), dma((8,)), dma((8,)), dma((8,)), dma((8,)), dma((8,)),
+            dma((8,)), dma((8,)), dma((8,)), dma((8,)), dma((8,)), dma((8,)), dma((full[0] // 8,)),
         ],
         compiler_params=pltpu.CompilerParams(
             collective_id=0, has_side_effects=True, vmem_limit_bytes=61 << 20
@@ -515,10 +570,17 @@
             jax.ShapeDtypeStruct(density.shape, F32),
             jax.ShapeDtypeStruct((3,) + density.shape, F32),
         ),
-        in_specs=[vmem],
-        out_specs=(vmem, vmem),
-        scratch_shapes=[pltpu.VMEM(full, F32), pltpu.VMEM(full, F32)],
-        compiler_params=pltpu.CompilerParams(vmem_limit_bytes=32 << 20),
+        in_specs=[hbm],
+        out_specs=(hbm, hbm),
+        scratch_shapes=[
+            pltpu.VMEM(full, F32),
+            pltpu.VMEM(full, F32),
+            pltpu.VMEM(full, F32),
+            pltpu.VMEM(density.shape, F32),
+            pltpu.VMEM((3,) + density.shape, F32),
+            dma((full[0] // 8,)), dma((size_x // 8,)), dma((size_x // 8,)),
+        ],
+        compiler_params=pltpu.CompilerParams(vmem_limit_bytes=61 << 20),
         name="finish",
     )(ext)
 

time: 50.4 us -> 43.4 us (0.86)
  the two profiles are of different devices: /device:TPU:153 before, /device:TPU:155 now
where the time goes in v3:
time: 43.4 us; the launch traced here: 43.2 us
  Pallas kernels  42.6 us (98%)
  between operations  0.64 us (1%)
    pallas_call x1, Pallas kernels, shards(): pl.pallas_call(blend_kernel, out_shape=jax.ShapeDtypeStruct(full, F32), i...  39.2 us
    pallas_call x1, Pallas kernels, shards(): pl.pallas_call(finish_kernel, out_shape=(jax.ShapeDtypeStruct(density.sha...  3.42 us

profile of v3, /device:TPU:155, one launch (start us, length us, event | category | flops | bytes accessed | tf_op | source)
XLA Modules:
  0.0 43.2 jit_solution(3892303502584110428)
XLA Ops:
  0.6 39.2 %blend.1.ext = f32[40,40,128]{2,1,0:T(8,128)} custom-call(f32[32,32,128]{2,1,0:T(8,128)} %dens.1, bf16[4,64,2048]{2,1,0:T(8,128)(2,1)} %bitcast.9, s32[4,2048]{1,0:T(4,128)} %bitcast.11, s32[1,4]{1,0:T(1,128)} %bitcast.15, bf16[64,256]{1,0:T(8,128)(2,1)} %bitcast.12, bf16[4,256,256]{2,1,0:T(8,128)(2,1)} %bitcast.10, bf16[1,256]{1,0:T(2,128)(2,1)} %bitcast.14, ...), custom_call_target="tpu_custom_call" | custom-call | tf_op jit(solution)/shard_map/blend/pallas_call | solution.py:520
  39.8 3.4 %finish.1 = (f32[32,32,128]{2,1,0:T(8,128)}, f32[3,32,32,128]{3,2,1,0:T(8,128)}) custom-call(f32[40,40,128]{2,1,0:T(8,128)} %blend.1.ext), custom_call_target="tpu_custom_call" | custom-call | tf_op jit(solution)/shard_map/finish/pallas_call | solution.py:567

commit v4 on v3

--- a/solution.py
+++ b/solution.py
@@ -11,7 +11,7 @@
 F32, BF16, I32 = jnp.float32, jnp.bfloat16, jnp.int32
 HX, HY = 4, 8
 GROUP = 4
-ROUTES = (2, 1, 2, 1, 0, 2, 1, 2)
+ROUTES = (2, 1, 3, 2, 0, 1, 3, 2)
 ROW_PARTS = 2
 AROUND = ((-1, 0), (1, 0), (0, -1), (0, 1), (-1, -1), (-1, 1), (1, -1), (1, 1))
 
@@ -270,10 +270,11 @@
         def _(s=s):
             feature_copy(s, *AROUND[s]).start()
 
-    for step, side, starts in reversed(flows):
+    lower = ix < nx // 2
+    for (step, side, starts), turn in ((flows[1], lower), (flows[0], True), (flows[1], jnp.logical_not(lower))):
         for n in range(len(ROUTES)):
             if ROUTES[n]:
-                @pl.when(starts(ROUTES[n] * step))
+                @pl.when(starts(ROUTES[n] * step) & turn)
                 def _(n=n, step=step, side=side):
                     far_copy(n, side, step).wait_recv()
                     forward_copy(n, side, step).start()
@@ -353,10 +354,12 @@
     lax.fori_loop(wide // 2 - pairs, wide // 2, prepare(own_groups), 0, unroll=True)
     lax.fori_loop(0, wide // 2, prepare((groups,)), 0, unroll=5)
 
-    for n, (dx, dy) in enumerate(AROUND):
-        @pl.when(there(-dx, -dy))
-        def _(n=n, dx=dx, dy=dy):
-            value_copy(n, dx, dy).wait_recv()
+    def arrived(along):
+        for n, (dx, dy) in enumerate(AROUND):
+            if -dx == along:
+                @pl.when(there(-dx, -dy))
+                def _(n=n, dx=dx, dy=dy):
+                    value_copy(n, dx, dy).wait_recv()
 
     def put(which, first, source):
         values[which, first : first + source.shape[0]] = source
@@ -366,36 +369,25 @@
     lo_3, hi_3 = base_3 + pairs, base_3 + pairs + rows
     west, east, south, north = (values_in.at[m] for m in range(4))
     south_west, north_west, south_east, north_east = (values_in.at[m] for m in range(4, 8))
-    put(0, HX, west[0:rows])
-    put(0, HX + rows, east[0:rows])
     put(0, 0, nets[1, rows - HX : rows])
     put(0, tail, nets[0, 0:HX])
+    put(1, lo_3, nets[3])
+    put(2, lo_2, nets[2])
+    arrived(0)
     put(0, lo_2, south[0:rows])
     put(0, lo_3, north[0:rows])
-    put(0, base_2, south_west[strip : strip + pairs])
-    put(0, base_3, north_west[strip + pairs : strip + 2 * pairs])
-    put(0, hi_2, south_east[strip : strip + pairs])
-    put(0, hi_3, north_east[strip + pairs : strip + 2 * pairs])
-    for which, column, to_west, to_east in ((1, south, south_west, south_east), (2, north, north_west, north_east)):
-        put(which, HX, to_west[0:rows])
-        put(which, HX + rows, to_east[0:rows])
+    for which, column in ((1, south), (2, north)):
         put(which, 0, column[strip + HX : strip + 2 * HX])
         put(which, tail, column[strip : strip + HX])
-    put(1, lo_3, nets[3])
-    put(1, base_3, west[strip + pairs : strip + 2 * pairs])
-    put(1, hi_3, east[strip + pairs : strip + 2 * pairs])
-    put(2, lo_2, nets[2])
-    put(2, base_2, west[strip : strip + pairs])
-    put(2, hi_2, east[strip : strip + pairs])
 
     def result_copy(chunk):
-        part = pl.ds(8 * chunk, 8)
+        part = pl.ds(4 * chunk, 4)
         return pltpu.make_async_copy(field.at[part], out.at[part], out_sem.at[chunk])
 
-    def blend(chunk, _):
-        for k in range(8):
-            pair, parity = 4 * chunk + k // 2, k % 2
-            x = 8 * chunk + k
+    def blend(chunk):
+        for k in range(4):
+            pair, parity = 2 * chunk + k // 2, k % 2
+            x = 4 * chunk + k
             for g in range(groups + 1):
                 from_x, from_y = entries(values, g, pair, parity)
                 voxels = pl.ds(8 * g, 8)
@@ -403,9 +395,42 @@
                     field[x, voxels, :] + coef_x[x, voxels, :] * from_x + coef_y[x, voxels, :] * from_y
                 )
         result_copy(chunk).start()
+
+    chunks = wide // 4
+
+    def blend_half(turn, _):
+        upper = jnp.where(place_in == 0, 1 - turn, turn)
+
+        @pl.when(upper == 0)
+        def _():
+            arrived(-1)
+            put(0, HX, west[0:rows])
+            put(0, base_2, south_west[strip : strip + pairs])
+            put(0, base_3, north_west[strip + pairs : strip + 2 * pairs])
+            put(1, HX, south_west[0:rows])
+            put(2, HX, north_west[0:rows])
+            put(1, base_3, west[strip + pairs : strip + 2 * pairs])
+            put(2, base_2, west[strip : strip + pairs])
+
+        @pl.when(upper == 1)
+        def _():
+            arrived(1)
+            put(0, HX + rows, east[0:rows])
+            put(0, hi_2, south_east[strip : strip + pairs])
+            put(0, hi_3, north_east[strip + pairs : strip + 2 * pairs])
+            put(1, HX + rows, south_east[0:rows])
+            put(2, HX + rows, north_east[0:rows])
+            put(1, hi_3, east[strip + pairs : strip + 2 * pairs])
+            put(2, hi_2, east[strip : strip + pairs])
+
+        def step(k, _):
+            blend(chunks // 2 * upper + k)
+            return 0
+
+        lax.fori_loop(0, chunks // 2, step, 0, unroll=True)
         return 0
 
-    lax.fori_loop(0, wide // 8, blend, 0)
+    lax.fori_loop(0, 2, blend_half, 0)
 
     for s in range(4):
         @pl.when(near(s))
@@ -430,7 +455,7 @@
             cell_copy(n, dx, dy).wait_send()
             density_copy(n, dx, dy).wait_send()
             value_copy(n, dx, dy).wait_send()
-    for chunk in range(wide // 8):
+    for chunk in range(chunks):
         result_copy(chunk).wait()
 
 
@@ -554,7 +579,7 @@
             pltpu.VMEM((2, len(ROUTES), width // ROW_PARTS, listed * ROW_PARTS // len(ROUTES)), BF16),
             dma((7,)), dma((len(ROUTES),)), dma((len(ROUTES),)), dma((2, len(ROUTES))), dma((2, len(ROUTES))),
             dma((sides,)), dma((sides,)),
-            dma((8,)), dma((8,)), dma((8,)), dma((8,)), dma((8,)), dma((8,)), dma((full[0] // 8,)),
+            dma((8,)), dma((8,)), dma((8,)), dma((8,)), dma((8,)), dma((8,)), dma((full[0] // 4,)),
         ],
         compiler_params=pltpu.CompilerParams(
             collective_id=0, has_side_effects=True, vmem_limit_bytes=61 << 20

time: 43.4 us -> 42.4 us (0.977)
  the two profiles are of different devices: /device:TPU:155 before, /device:TPU:27 now
where the time goes in v4:
time: 42.4 us; the launch traced here: 42.2 us
  Pallas kernels  41.6 us (98%)
  between operations  0.64 us (2%)
    pallas_call x1, Pallas kernels, shards(): pl.pallas_call(blend_kernel, out_shape=jax.ShapeDtypeStruct(full, F32), i...  38.2 us
    pallas_call x1, Pallas kernels, shards(): pl.pallas_call(finish_kernel, out_shape=(jax.ShapeDtypeStruct(density.sha...  3.42 us

profile of v4, /device:TPU:27, one launch (start us, length us, event | category | flops | bytes accessed | tf_op | source)
XLA Modules:
  0.0 42.2 jit_solution(2964321000688159142)
XLA Ops:
  0.6 38.2 %blend.1.ext = f32[40,40,128]{2,1,0:T(8,128)} custom-call(f32[32,32,128]{2,1,0:T(8,128)} %dens.1, bf16[4,64,2048]{2,1,0:T(8,128)(2,1)} %bitcast.9, s32[4,2048]{1,0:T(4,128)} %bitcast.11, s32[1,4]{1,0:T(1,128)} %bitcast.15, bf16[64,256]{1,0:T(8,128)(2,1)} %bitcast.12, bf16[4,256,256]{2,1,0:T(8,128)(2,1)} %bitcast.10, bf16[1,256]{1,0:T(2,128)(2,1)} %bitcast.14, ...), custom_call_target="tpu_custom_call" | custom-call | tf_op jit(solution)/shard_map/blend/pallas_call | solution.py:545
  38.8 3.4 %finish.1 = (f32[32,32,128]{2,1,0:T(8,128)}, f32[3,32,32,128]{3,2,1,0:T(8,128)}) custom-call(f32[40,40,128]{2,1,0:T(8,128)} %blend.1.ext), custom_call_target="tpu_custom_call" | custom-call | tf_op jit(solution)/shard_map/finish/pallas_call | solution.py:592

commit v5 on v4

--- a/solution.py
+++ b/solution.py
@@ -24,7 +24,7 @@
 def blend_kernel(
     dens, feat, cell, count, w_in, w_hid, w_out, bias, out,
     field, side_after, side_before, coef_x, coef_y, recv, cells, tile_lo, tile_hi, tiles_in, cells_in, table,
-    nets, up, down, left, right, values_in, values,
+    nets, up, down, left, right, corner_out, corner_in, values_in, values,
     cell_v, count_s, win_v, whid_v, wout_v, bias_v, win_t, whid_t, bias_w,
     relayed, load_sem, far_send, far_recv, relay_send, relay_recv, feat_send, feat_recv, dens_send, dens_recv, cell_send, cell_recv, value_send, value_recv, out_sem,
 ):
@@ -56,6 +56,7 @@
     side_after[...] = jnp.zeros_like(side_after)
     side_before[...] = jnp.zeros_like(side_before)
     values_in[...] = jnp.zeros_like(values_in)
+    corner_in[...] = jnp.zeros_like(corner_in)
     nets[...] = jnp.zeros_like(nets)
     tiles_in[...] = jnp.full_like(tiles_in, -1)
     cells_in[...] = jnp.full_like(cells_in, -1)
@@ -226,6 +227,8 @@
 
     def value_copy(n, dx, dy):
         m = AROUND.index((-dx, -dy))
+        if dx and dy:
+            return remote(corner_out.at[n - 4], corner_in.at[m - 4], value_send, value_recv, n, dx, dy)
         src = (left if dy < 0 else right) if dx == 0 else (down if dx < 0 else up)
         return remote(src, values_in.at[m], value_send, value_recv, n, dx, dy)
 
@@ -334,6 +337,35 @@
     for side in (left, right):
         side[rows : rows + HX] = nets[0, 0:HX]
         side[rows + HX : rows + 2 * HX] = nets[1, rows - HX : rows]
+    first_half = lax.broadcasted_iota(I32, (1, 128), 1) < 64
+    for n in range(4, 8):
+        dx, dy = AROUND[n]
+        along, beside = (0 if dx > 0 else 1), (2 if dy > 0 else 3)
+        edge = 4 * HX
+        shift = 128 - edge if dy > 0 else edge
+        near_edge = lane >= 128 - edge if dy > 0 else lane < edge
+        corner_out[n - 4] = jnp.where(near_edge, nets[along, 0:8], pltpu.roll(nets[along, 8:16], shift, 1))
+        for k in range(pairs):
+            at_row = rows - pairs + k if dx > 0 else k
+            line = nets[beside, at_row : at_row + 1, :]
+            turned = pltpu.roll(line, 64, 1)
+            kept = first_half if dy > 0 else jnp.logical_not(first_half)
+            for h, value in enumerate((line, turned) if dy > 0 else (turned, line)):
+                to = 2 * k + h
+                corner_out[n - 4, to : to + 1, :] = jnp.where(kept, value, corner_out[n - 4, to : to + 1, :])
+
+    def unpacked(m):
+        tile = corner_in[m - 4]
+        low = AROUND[m][1] < 0
+        lines = []
+        for k in range(pairs):
+            one, two = tile[2 * k : 2 * k + 1], tile[2 * k + 1 : 2 * k + 2]
+            if low:
+                lines.append(jnp.where(first_half, one, pltpu.roll(two, 64, 1)))
+            else:
+                lines.append(jnp.where(first_half, pltpu.roll(one, 64, 1), two))
+        return tile, pltpu.roll(tile, 4 * HX if low else 128 - 4 * HX, 1), lines
+
     for n, (dx, dy) in enumerate(AROUND):
         @pl.when(there(dx, dy))
         def _(n=n, dx=dx, dy=dy):
@@ -368,7 +400,14 @@
     lo_2, hi_2 = base_2 + pairs, base_2 + pairs + rows
     lo_3, hi_3 = base_3 + pairs, base_3 + pairs + rows
     west, east, south, north = (values_in.at[m] for m in range(4))
-    south_west, north_west, south_east, north_east = (values_in.at[m] for m in range(4, 8))
+
+    def put_corner(m, which, base, at_x, at_pair):
+        head_rows, tail_rows, lines = unpacked(m)
+        put(which, at_x, head_rows)
+        put(which, at_x + 8, tail_rows)
+        for k, line in enumerate(lines):
+            put(0, base + at_pair + k, line)
+
     put(0, 0, nets[1, rows - HX : rows])
     put(0, tail, nets[0, 0:HX])
     put(1, lo_3, nets[3])
@@ -405,10 +444,8 @@
         def _():
             arrived(-1)
             put(0, HX, west[0:rows])
-            put(0, base_2, south_west[strip : strip + pairs])
-            put(0, base_3, north_west[strip + pairs : strip + 2 * pairs])
-            put(1, HX, south_west[0:rows])
-            put(2, HX, north_west[0:rows])
+            put_corner(4, 1, base_2, HX, 0)
+            put_corner(5, 2, base_3, HX, 0)
             put(1, base_3, west[strip + pairs : strip + 2 * pairs])
             put(2, base_2, west[strip : strip + pairs])
 
@@ -416,10 +453,8 @@
         def _():
             arrived(1)
             put(0, HX + rows, east[0:rows])
-            put(0, hi_2, south_east[strip : strip + pairs])
-            put(0, hi_3, north_east[strip + pairs : strip + 2 * pairs])
-            put(1, HX + rows, south_east[0:rows])
-            put(2, HX + rows, north_east[0:rows])
+            put_corner(6, 1, base_2, HX + rows, pairs + rows)
+            put_corner(7, 2, base_3, HX + rows, pairs + rows)
             put(1, hi_3, east[strip + pairs : strip + 2 * pairs])
             put(2, hi_2, east[strip : strip + pairs])
 
@@ -565,7 +600,9 @@
             pltpu.VMEM(message, F32),
             pltpu.VMEM(message, F32),
             pltpu.VMEM(message, F32),
-            pltpu.VMEM((8,) + message, F32),
+            pltpu.VMEM((4, 8, 128), F32),
+            pltpu.VMEM((4, 8, 128), F32),
+            pltpu.VMEM((4,) + message, F32),
             pltpu.VMEM(tables, F32),
             pltpu.VMEM((sides, listed), I32),
             pltpu.SMEM((1, sides), I32),

time: 42.4 us -> 41.8 us (0.986)
  the two profiles are of different devices: /device:TPU:27 before, /device:TPU:151 now
where the time goes in v5:
time: 41.8 us; the launch traced here: 41.6 us
  Pallas kernels  41 us (98%)
  between operations  0.64 us (2%)
    pallas_call x1, Pallas kernels, shards(): pl.pallas_call(blend_kernel, out_shape=jax.ShapeDtypeStruct(full, F32), i...  37.6 us
    pallas_call x1, Pallas kernels, shards(): pl.pallas_call(finish_kernel, out_shape=(jax.ShapeDtypeStruct(density.sha...  3.42 us

profile of v5, /device:TPU:151, one launch (start us, length us, event | category | flops | bytes accessed | tf_op | source)
XLA Modules:
  0.0 41.6 jit_solution(15806069223989796006)
XLA Ops:
  0.6 37.6 %blend.1.ext = f32[40,40,128]{2,1,0:T(8,128)} custom-call(f32[32,32,128]{2,1,0:T(8,128)} %dens.1, bf16[4,64,2048]{2,1,0:T(8,128)(2,1)} %bitcast.9, s32[4,2048]{1,0:T(4,128)} %bitcast.11, s32[1,4]{1,0:T(1,128)} %bitcast.15, bf16[64,256]{1,0:T(8,128)(2,1)} %bitcast.12, bf16[4,256,256]{2,1,0:T(8,128)(2,1)} %bitcast.10, bf16[1,256]{1,0:T(2,128)(2,1)} %bitcast.14, ...), custom_call_target="tpu_custom_call" | custom-call | tf_op jit(solution)/shard_map/blend/pallas_call | solution.py:580
  38.2 3.4 %finish.1 = (f32[32,32,128]{2,1,0:T(8,128)}, f32[3,32,32,128]{3,2,1,0:T(8,128)}) custom-call(f32[40,40,128]{2,1,0:T(8,128)} %blend.1.ext), custom_call_target="tpu_custom_call" | custom-call | tf_op jit(solution)/shard_map/finish/pallas_call | solution.py:629

commit v6 on v5

--- a/solution.py
+++ b/solution.py
@@ -329,14 +329,17 @@
 
     up[0:rows] = nets[0]
     down[0:rows] = nets[1]
-    left[0:rows] = nets[3]
-    right[0:rows] = nets[2]
     for n, s in enumerate((2, 3)):
         up[rows + n * pairs : rows + (n + 1) * pairs] = nets[s, rows - pairs : rows]
         down[rows + n * pairs : rows + (n + 1) * pairs] = nets[s, 0:pairs]
-    for side in (left, right):
-        side[rows : rows + HX] = nets[0, 0:HX]
-        side[rows + HX : rows + 2 * HX] = nets[1, rows - HX : rows]
+
+    def send_values(chosen):
+        for n in chosen:
+            @pl.when(there(*AROUND[n]))
+            def _(n=n):
+                value_copy(n, *AROUND[n]).start()
+
+    send_values((0, 1))
     first_half = lax.broadcasted_iota(I32, (1, 128), 1) < 64
     for n in range(4, 8):
         dx, dy = AROUND[n]
@@ -354,6 +357,14 @@
                 to = 2 * k + h
                 corner_out[n - 4, to : to + 1, :] = jnp.where(kept, value, corner_out[n - 4, to : to + 1, :])
 
+    send_values((4, 5, 6, 7))
+    left[0:rows] = nets[3]
+    right[0:rows] = nets[2]
+    for side in (left, right):
+        side[rows : rows + HX] = nets[0, 0:HX]
+        side[rows + HX : rows + 2 * HX] = nets[1, rows - HX : rows]
+    send_values((2, 3))
+
     def unpacked(m):
         tile = corner_in[m - 4]
         low = AROUND[m][1] < 0
@@ -365,11 +376,6 @@
             else:
                 lines.append(jnp.where(first_half, pltpu.roll(one, 64, 1), two))
         return tile, pltpu.roll(tile, 4 * HX if low else 128 - 4 * HX, 1), lines
-
-    for n, (dx, dy) in enumerate(AROUND):
-        @pl.when(there(dx, dy))
-        def _(n=n, dx=dx, dy=dy):
-            value_copy(n, dx, dy).start()
 
     for n, (dx, dy) in enumerate(AROUND):
         @pl.when(there(-dx, -dy))

time: 41.8 us -> 41.7 us (level)
  the two profiles are of different devices: /device:TPU:151 before, /device:TPU:159 now
where the time goes in v6:
time: 41.7 us; the launch traced here: 41.6 us
  Pallas kernels  40.9 us (98%)
  between operations  0.64 us (2%)
    pallas_call x1, Pallas kernels, shards(): pl.pallas_call(blend_kernel, out_shape=jax.ShapeDtypeStruct(full, F32), i...  37.5 us
    pallas_call x1, Pallas kernels, shards(): pl.pallas_call(finish_kernel, out_shape=(jax.ShapeDtypeStruct(density.sha...  3.42 us

profile of v6, /device:TPU:159, one launch (start us, length us, event | category | flops | bytes accessed | tf_op | source)
XLA Modules:
  0.0 41.6 jit_solution(3555442911511753053)
XLA Ops:
  0.6 37.5 %blend.1.ext = f32[40,40,128]{2,1,0:T(8,128)} custom-call(f32[32,32,128]{2,1,0:T(8,128)} %dens.1, bf16[4,64,2048]{2,1,0:T(8,128)(2,1)} %bitcast.9, s32[4,2048]{1,0:T(4,128)} %bitcast.11, s32[1,4]{1,0:T(1,128)} %bitcast.15, bf16[64,256]{1,0:T(8,128)(2,1)} %bitcast.12, bf16[4,256,256]{2,1,0:T(8,128)(2,1)} %bitcast.10, bf16[1,256]{1,0:T(2,128)(2,1)} %bitcast.14, ...), custom_call_target="tpu_custom_call" | custom-call | tf_op jit(solution)/shard_map/blend/pallas_call | solution.py:586
  38.1 3.4 %finish.1 = (f32[32,32,128]{2,1,0:T(8,128)}, f32[3,32,32,128]{3,2,1,0:T(8,128)}) custom-call(f32[40,40,128]{2,1,0:T(8,128)} %blend.1.ext), custom_call_target="tpu_custom_call" | custom-call | tf_op jit(solution)/shard_map/finish/pallas_call | solution.py:635
